TPU v7x, 32 devices: a whole 2x2x4 slice. The times are simulated.
32 devices in a mesh: groups: 2 (over y), tensor: 16 (over z, x, core).
Axes of the slice: x: 2, y: 2, z: 4, core: 2. Of those that a mesh axis runs over, the one named last changes fastest.
Arguments:
- tapped: bfloat16 [256, 49152], P('groups', 'tensor'), parts along dimension 0, may hold values from -6 to 6
- join_weight: bfloat16 [49152, 8192], P('tensor'), may hold values from -0.02734375 to 0.02734375
- norm_gain: float32 [8192], replicated, may hold values from 0.25 to 1.75
- query_weight: bfloat16 [8192, 8192], P(None, 'tensor'), may hold values from -0.0625 to 0.0625
- kv_weight: bfloat16 [8192, 2048], P(None, 'tensor'), may hold values from -0.0625 to 0.0625
- out_weight: bfloat16 [8192, 8192], P('tensor'), may hold values from -0.0625 to 0.0625
- kv_cache: bfloat16 [4, 262144, 256], P('groups', 'tensor'), parts along dimension 0, may hold values from -360 to 360
- lengths: int32 [4], P('groups'), parts along dimension 0, may hold values from 1 to 32768, as said below
- parents: int32 [2, 256], P(None, 'groups'), parts along dimension 1, may hold values from 0 to 63
Outputs:
- draft_hidden: float32 [256, 8192], P(('groups', 'tensor')), parts along dimension 0
There are 2 independent parts, one for each index of `groups`. A program takes and returns all parts, laid end to end along the dimension named above; an argument that names none is the same for every part. Nothing has to cross between parts.
Inputs may be any that keep to these rules, and one draw needn't show every extreme that they name: `lengths`: every sequence has at least one cached token, and in every part one sequence has exactly 32768. `parents`: node numbers within the row's sequence.
All inputs are finite; a program needn't handle non-finite values.
Results may differ from a plain program's by a relative error of at most 0.03.
Values may be sent and summed in bfloat16 or wider, within the bound.
No kernel may reach another device: no remote copies, remote signals or barrier semaphores. Data moves between devices by JAX's collectives and lax.ppermute only.
A program may use at most 384 MiB of HBM per device.

v0:
```python
import functools
import math

import jax
import jax.numpy as jnp
from jax import lax
from jax.experimental import pallas as pl
from jax.experimental.pallas import tpu as pltpu
from jax.sharding import PartitionSpec as P

KVH = 8
HD = 128
QPK = 8
STEPS = 3


epsilon = 1e-05
floor_score = -1e30


def partner(x, axis, distance):
    return lax.ppermute(x, axis, [(i, i ^ 1 << distance) for i in range(lax.axis_size(axis))])


def as_sent(x):

    def short(part):
        return part.astype(jnp.bfloat16) if part.dtype == jnp.float32 else part

    return jax.tree.map(short, x)


def normalize(values, norm_gain):
    mean_square = jnp.mean(values * values, axis=-1, keepdims=True)
    return (values * lax.rsqrt(mean_square + epsilon) * norm_gain).astype(jnp.bfloat16)


def merge_parts(mine, theirs):
    row_top = jnp.maximum(mine[0], theirs[0])
    mine_factor = jnp.exp(mine[0] - row_top)
    their_factor = jnp.exp(theirs[0] - row_top)
    row_sum = mine_factor * mine[1] + their_factor * theirs[1]
    numerator = mine_factor[..., None] * mine[2] + their_factor[..., None] * theirs[2]
    return (row_top, row_sum, numerator)


def local_general(
    tapped, join_weight, norm_gain, query_weight, kv_weight, out_weight, kv_cache, lengths, parents
):
    tensor_size = lax.axis_size("tensor")
    device = lax.axis_index("tensor")
    group_size = tensor_size // KVH
    hop_count = group_size.bit_length() - 1
    piece_index = device % group_size
    row_count_all = tapped.shape[0]
    seq_count = kv_cache.shape[0]
    node_count = row_count_all // seq_count
    query_cols = query_weight.shape[1]
    proj_weight = jnp.concatenate([query_weight, kv_weight], axis=1)
    score_scale = 1.0 / math.sqrt(HD)
    hidden_rows = lax.psum_scatter(
        jnp.dot(tapped, join_weight, preferred_element_type=jnp.float32),
        "tensor",
        scatter_dimension=0,
        tiled=True,
    )
    piece_len = kv_cache.shape[1]
    positions = piece_index * piece_len + jnp.arange(piece_len, dtype=jnp.int32)
    visible = positions[None, :] < lengths[:, None]
    is_first = piece_index == 0
    keys_cache = kv_cache[:, :, :HD]
    values_cache = kv_cache[:, :, HD:]
    row_ids = jnp.arange(row_count_all, dtype=jnp.int32)
    seq_base = row_ids // node_count * node_count
    head_rows = node_count * QPK
    width = out_weight.shape[0]
    history = []
    for step_num in range(STEPS):
        projected = jnp.dot(
            lax.all_gather(normalize(hidden_rows, norm_gain), "tensor", axis=0, tiled=True),
            proj_weight,
            preferred_element_type=jnp.float32,
        ).astype(jnp.bfloat16)
        query_group = projected[:, :query_cols]
        kv_group = projected[:, query_cols:]
        for bit_num in range(hop_count):
            other_query, other_kv = partner((query_group, kv_group), "tensor", bit_num)
            is_upper = device // (1 << bit_num) % 2 == 1
            query_group = jnp.where(
                is_upper,
                jnp.concatenate([other_query, query_group], axis=1),
                jnp.concatenate([query_group, other_query], axis=1),
            )
            kv_group = jnp.where(
                is_upper,
                jnp.concatenate([other_kv, kv_group], axis=1),
                jnp.concatenate([kv_group, other_kv], axis=1),
            )
        history.append(kv_group)
        ancestors = [row_ids]
        current = row_ids
        for earlier in range(step_num - 1, -1, -1):
            current = seq_base + jnp.take(parents[earlier], current, axis=0)
            ancestors.insert(0, current)
        new_depth = step_num + 1
        new_kv = jnp.stack(
            [
                jnp.take(history[earlier], ancestors[earlier], axis=0)
                for earlier in range(new_depth)
            ],
            axis=1,
        )
        new_keys = new_kv[..., :HD].reshape(seq_count, node_count, new_depth, HD)
        new_values = new_kv[..., HD:].reshape(seq_count, node_count, new_depth, HD)
        query_blocks = query_group.reshape(seq_count, head_rows, HD)
        scores = (
            jnp.einsum("brd,bcd->brc", query_blocks, keys_cache, preferred_element_type=jnp.float32)
            * score_scale
        )
        scores = jnp.where(visible[:, None, :], scores, floor_score)
        query_nodes = query_group.reshape(seq_count, node_count, QPK, HD)
        new_scores = (
            jnp.einsum("bnqd,bntd->bnqt", query_nodes, new_keys, preferred_element_type=jnp.float32)
            * score_scale
        )
        new_scores = jnp.where(is_first, new_scores, floor_score)
        row_top = jnp.maximum(
            jnp.max(scores, axis=-1), jnp.max(new_scores, axis=-1).reshape(seq_count, head_rows)
        )
        weights = jnp.where(visible[:, None, :], jnp.exp(scores - row_top[..., None]), 0.0)
        top_nodes = row_top.reshape(seq_count, node_count, QPK)
        new_weights = jnp.where(is_first, jnp.exp(new_scores - top_nodes[..., None]), 0.0)
        row_sum = jnp.sum(weights, axis=-1) + jnp.sum(new_weights, axis=-1).reshape(
            seq_count, head_rows
        )
        numerator = jnp.einsum(
            "brc,bcd->brd",
            weights.astype(jnp.bfloat16),
            values_cache,
            preferred_element_type=jnp.float32,
        )
        new_part = jnp.einsum(
            "bnqt,bntd->bnqd",
            new_weights.astype(jnp.bfloat16),
            new_values,
            preferred_element_type=jnp.float32,
        )
        numerator = numerator + new_part.reshape(seq_count, head_rows, HD)
        partial_value = (row_top, row_sum, numerator)
        for bit_num in range(hop_count):
            theirs = partner(
                (as_sent(partial_value[0]), as_sent(partial_value[1]), as_sent(partial_value[2])),
                "tensor",
                bit_num,
            )
            partial_value = merge_parts(partial_value, theirs)
        attended = (
            (partial_value[2] / partial_value[1][..., None])
            .astype(jnp.bfloat16)
            .reshape(row_count_all, QPK * HD)
        )
        attended_mine = lax.dynamic_slice_in_dim(attended, piece_index * width, width, 1)
        hidden_rows = hidden_rows + lax.psum_scatter(
            jnp.dot(attended_mine, out_weight, preferred_element_type=jnp.float32),
            "tensor",
            scatter_dimension=0,
            tiled=True,
        )
    return hidden_rows


BLOCK = 2048
SUB = BLOCK // 2
CHUNK = 256
TO_LOG2 = math.log2(math.e) / math.sqrt(HD)


def score_dot(query, key):
    return lax.dot_general(
        query, key, (((1,), (1,)), ((), ())), preferred_element_type=jnp.float32
    )


def wide(x, width):
    return jnp.concatenate([x] * (width // HD), axis=1)


def attend_kernel(depth, info_ref, mine_ref, other_ref, *refs):
    key_refs, value_refs, bias_refs = refs[:depth], refs[depth:2 * depth], refs[2 * depth:3 * depth]
    cache_ref, keep_ref, keep_lse_ref, send_ref, query_s = refs[3 * depth:3 * depth + 5]
    score_s, weight_s = refs[3 * depth + 5:3 * depth + 7], refs[3 * depth + 7:3 * depth + 9]
    top_s, sum_s, cache_s, live_s, sems = refs[3 * depth + 9:]
    seq_count = cache_ref.shape[0]
    node_count = mine_ref.shape[0] // seq_count
    half_heads = mine_ref.shape[1] // HD
    seq_rows = 2 * half_heads * node_count
    half_rows = seq_rows // 2
    slots = cache_s.shape[0]
    steps = [lax.div(info_ref[b] + BLOCK - 1, BLOCK) for b in range(seq_count)]
    total = sum(steps)

    def place(i):
        seq = jnp.int32(0)
        block = i
        for b in range(seq_count - 1):
            later = jnp.logical_and(block >= steps[b], seq == b)
            seq = jnp.where(later, b + 1, seq)
            block = jnp.where(later, block - steps[b], block)
        return seq, block

    def left_of(i):
        seq, block = place(i)
        return info_ref[seq] - block * BLOCK

    def fetch(i):
        seq, block = place(i)
        slot = lax.rem(i, slots)
        start = pl.multiple_of(block * BLOCK, BLOCK)
        return pltpu.make_async_copy(
            cache_ref.at[seq, pl.ds(start, BLOCK), :], cache_s.at[slot], sems.at[slot]
        )

    for i in range(2):
        pl.when(i < total)(lambda i=i: fetch(jnp.int32(i)).start())

    for b in range(seq_count):
        rows = slice(b * node_count, (b + 1) * node_count)
        for h in range(2 * half_heads):
            ref = mine_ref if h < half_heads else other_ref
            col = h % half_heads * HD
            row = b * seq_rows + h * node_count
            query_s[row:row + node_count, :] = ref[rows, col:col + HD]
    live_s[0] = jnp.ones((BLOCK, HD), jnp.bfloat16)

    @pl.when(info_ref[seq_count] == 0)
    def _():
        top_s[...] = jnp.full(top_s.shape, floor_score, jnp.float32)
        sum_s[...] = jnp.zeros(sum_s.shape, jnp.float32)

    @pl.when(info_ref[seq_count] != 0)
    def _():
        for b in range(seq_count):
            rows = slice(b * seq_rows, (b + 1) * seq_rows)
            query = query_s[rows, :]
            scores = []
            for t in range(depth):
                bias = bias_refs[t][b * node_count:(b + 1) * node_count, :]
                score = score_dot(query, key_refs[t][...])
                scores.append(score * TO_LOG2 + jnp.concatenate([bias] * (2 * half_heads), axis=0))
            top = functools.reduce(jnp.maximum, scores)
            top = jnp.broadcast_to(jnp.max(top, axis=1, keepdims=True), top.shape)
            gathered = jnp.zeros((seq_rows, 2 * HD), jnp.float32)
            for t in range(depth):
                weight = jnp.exp2(scores[t] - top).astype(jnp.bfloat16)
                value = value_refs[t][...]
                value = jnp.concatenate([value, jnp.ones_like(value)], axis=1)
                gathered = gathered + jnp.dot(weight, value, preferred_element_type=jnp.float32)
            top_s[rows, :] = top
            sum_s[rows, :] = gathered

    def patch(i):
        left = left_of(i)
        slot = lax.rem(i, slots)

        @pl.when(left < BLOCK)
        def _():
            inside = lax.broadcasted_iota(jnp.int32, (BLOCK, HD), 0) < left
            key = cache_s[slot, :, :HD].astype(jnp.float32)
            value = cache_s[slot, :, HD:].astype(jnp.float32)
            key = jnp.where(inside, key, jnp.broadcast_to(key[:1, :], key.shape))
            cache_s[slot, :, :HD] = key.astype(jnp.bfloat16)
            cache_s[slot, :, HD:] = jnp.where(inside, value, 0.0).astype(jnp.bfloat16)

    def score_chunk(seq, slot, sub, c):
        rows = pl.ds(pl.multiple_of(seq * seq_rows, seq_rows), seq_rows)
        at = sub * SUB + c
        score_s[sub][:, c:c + CHUNK] = score_dot(query_s[rows, :], cache_s[slot, at:at + CHUNK, :HD])

    def weigh(seq, slot, part, sub, half, between):
        rows = pl.ds(pl.multiple_of(seq * seq_rows + half * half_rows, half_rows), half_rows)
        here = slice(half * half_rows, (half + 1) * half_rows)
        high = score_s[sub][here, :HD]
        for c in range(HD, SUB, HD):
            high = jnp.maximum(high, score_s[sub][here, c:c + HD])
        high = jnp.broadcast_to(jnp.max(high, axis=1, keepdims=True), high.shape) * TO_LOG2
        old = top_s[rows, :]
        top = jnp.maximum(old, high)
        top_s[rows, :] = top
        factor = jnp.exp2(old - top)
        between[0]()
        tops = wide(top, CHUNK)
        for c in range(0, SUB, CHUNK):
            weight = jnp.exp2(score_s[sub][here, c:c + CHUNK] * TO_LOG2 - tops)
            weight_s[sub][here, c:c + CHUNK] = weight.astype(jnp.bfloat16)
            if c == SUB // 2:
                between[1]()
        keys = slice(sub * SUB, (sub + 1) * SUB)
        value = jnp.concatenate([cache_s[slot, keys, HD:], live_s[part, keys, :]], axis=1)
        sum_s[rows, :] = sum_s[rows, :] * wide(factor, 2 * HD) + jnp.dot(
            weight_s[sub][here, :], value, preferred_element_type=jnp.float32
        )

    def phase(seq, slot, part, sub, next_seq, next_slot):
        ahead = [
            functools.partial(score_chunk, next_seq, next_slot, 1 - sub, c)
            for c in range(0, SUB, CHUNK)
        ]
        weigh(seq, slot, part, sub, 0, ahead[:2])
        weigh(seq, slot, part, sub, 1, ahead[2:])

    @pl.when(total > 0)
    def _():
        fetch(jnp.int32(0)).wait()
        patch(jnp.int32(0))
        seq, _ = place(jnp.int32(0))
        for c in range(0, SUB, CHUNK):
            score_chunk(seq, 0, 0, c)

    @pl.loop(0, total)
    def _(i):
        slot = lax.rem(i, slots)
        more = i + 1 < total

        @pl.when(more)
        def _():
            fetch(i + 1).wait()
            patch(i + 1)

        pl.when(i + 2 < total)(lambda: fetch(i + 2).start())
        seq, _ = place(i)
        left = left_of(i)
        part = jnp.where(left < BLOCK, 1, 0)

        @pl.when(left < BLOCK)
        def _():
            inside = lax.broadcasted_iota(jnp.int32, (BLOCK, HD), 0) < left
            live_s[1] = jnp.where(inside, 1.0, 0.0).astype(jnp.bfloat16)

        next_slot = jnp.where(more, lax.rem(i + 1, slots), slot)
        next_seq, _ = place(jnp.where(more, i + 1, i))
        phase(seq, slot, part, 0, seq, slot)
        phase(seq, slot, part, 1, next_seq, next_slot)

    for b in range(seq_count):
        rows = slice(b * node_count, (b + 1) * node_count)
        for h in range(2 * half_heads):
            row = b * seq_rows + h * node_count
            weight_sum = jnp.maximum(sum_s[row:row + node_count, HD:], 1e-30)
            result = sum_s[row:row + node_count, :HD] / weight_sum
            lse = top_s[row:row + node_count, :] + jnp.log2(weight_sum)
            col = h % half_heads * HD
            if h < half_heads:
                keep_ref[rows, col:col + HD] = result
                keep_lse_ref[rows, col:col + HD] = lse
            else:
                send_ref[rows, col:col + HD] = result
                send_ref[rows, half_heads * HD + col:half_heads * HD + col + HD] = lse


def attend(info, mine, other, keys, values, biases, cache):
    depth = len(keys)
    row_count, width = mine.shape
    seq_count, slot_count = cache.shape[:2]
    all_rows = 2 * width // HD * row_count
    seq_rows = all_rows // seq_count
    vmem = pl.BlockSpec(memory_space=pltpu.VMEM)
    return pl.pallas_call(
        functools.partial(attend_kernel, depth),
        out_shape=(
            jax.ShapeDtypeStruct((row_count, width), jnp.float32),
            jax.ShapeDtypeStruct((row_count, width), jnp.float32),
            jax.ShapeDtypeStruct((row_count, 2 * width), jnp.float32),
        ),
        in_specs=[pl.BlockSpec(memory_space=pltpu.SMEM)]
        + [vmem] * (2 + 3 * depth)
        + [pl.BlockSpec(memory_space=pltpu.HBM)],
        out_specs=(vmem, vmem, vmem),
        scratch_shapes=[
            pltpu.VMEM((all_rows, HD), jnp.bfloat16),
            pltpu.VMEM((seq_rows, SUB), jnp.float32),
            pltpu.VMEM((seq_rows, SUB), jnp.float32),
            pltpu.VMEM((seq_rows, SUB), jnp.bfloat16),
            pltpu.VMEM((seq_rows, SUB), jnp.bfloat16),
            pltpu.VMEM((all_rows, HD), jnp.float32),
            pltpu.VMEM((all_rows, 2 * HD), jnp.float32),
            pltpu.VMEM((3, BLOCK, 2 * HD), jnp.bfloat16),
            pltpu.VMEM((2, BLOCK, HD), jnp.bfloat16),
            pltpu.SemaphoreType.DMA((3,)),
        ],
        compiler_params=pltpu.CompilerParams(vmem_limit_bytes=24 * 1024 * 1024),
        cost_estimate=pl.CostEstimate(
            flops=4 * all_rows * slot_count * HD,
            bytes_accessed=2 * cache.size,
            transcendentals=all_rows * slot_count,
        ),
        name="attend",
    )(
        info, mine, other, *keys, *values, *biases,
        pltpu.with_memory_space_constraint(cache, pltpu.HBM),
    )


STRIP = 256
STRIPS = 4
TILE = 512


def join_kernel(start, side_ref, x_ref, weight_ref, keep_ref, send_ref, x_s, strip_s, total_s, x_sem, sems):
    side = side_ref[0]
    depth = x_s.shape[1]
    columns = total_s.shape[1]
    count = depth // STRIP
    own = 8

    def strip(i):
        slot = lax.rem(i, STRIPS)
        rows = pl.ds(pl.multiple_of(i * STRIP, STRIP), STRIP)
        return pltpu.make_async_copy(
            weight_ref.at[rows, pl.ds(start, columns)], strip_s.at[slot], sems.at[slot]
        )

    x_copy = pltpu.make_async_copy(x_ref, x_s, x_sem)
    x_copy.start()
    for i in range(STRIPS - 1):
        strip(jnp.int32(i)).start()
    total_s[...] = jnp.zeros(total_s.shape, jnp.float32)
    x_copy.wait()

    @pl.loop(0, count)
    def _(i):
        slot = lax.rem(i, STRIPS)
        pl.when(i + STRIPS - 1 < count)(lambda: strip(i + STRIPS - 1).start())
        strip(i).wait()
        x = x_s[:, pl.ds(pl.multiple_of(i * STRIP, STRIP), STRIP)]
        for c in range(0, columns, TILE):
            total_s[:, c:c + TILE] += jnp.dot(
                x, strip_s[slot, :, c:c + TILE], preferred_element_type=jnp.float32
            )

    for block in range(keep_ref.shape[0] // own):
        rows = slice(block * own, (block + 1) * own)
        keep_at = pl.multiple_of(2 * block * own + side * own, own)
        send_at = pl.multiple_of(2 * block * own + (1 - side) * own, own)
        keep_ref[rows, :] = total_s[pl.ds(keep_at, own), :]
        send_ref[rows, :] = total_s[pl.ds(send_at, own), :]


def join(side, x, weight, start, columns):
    rows, depth = x.shape
    out = jax.ShapeDtypeStruct((rows // 2, columns), jnp.float32)
    vmem = pl.BlockSpec(memory_space=pltpu.VMEM)
    return pl.pallas_call(
        functools.partial(join_kernel, start),
        out_shape=(out, out),
        in_specs=[
            pl.BlockSpec(memory_space=pltpu.SMEM),
            pl.BlockSpec(memory_space=pl.ANY),
            pl.BlockSpec(memory_space=pl.ANY),
        ],
        out_specs=(vmem, vmem),
        scratch_shapes=[
            pltpu.VMEM((rows, depth), x.dtype),
            pltpu.VMEM((STRIPS, STRIP, columns), weight.dtype),
            pltpu.VMEM((rows, columns), jnp.float32),
            pltpu.SemaphoreType.DMA,
            pltpu.SemaphoreType.DMA((STRIPS,)),
        ],
        compiler_params=pltpu.CompilerParams(vmem_limit_bytes=32 * 1024 * 1024),
        cost_estimate=pl.CostEstimate(
            flops=2 * rows * depth * columns, bytes_accessed=2 * depth * columns, transcendentals=0
        ),
        name="join",
    )(side[None], x, weight)


CORE, ACROSS, DEEP = range(3)


def bit_of(distance):
    return lax.axis_index("tensor") // (1 << distance) % 2


def fold(x, axis, distance, kind=jnp.bfloat16):
    bit = bit_of(distance)
    keep = lax.dynamic_index_in_dim(x, bit, axis, keepdims=False)
    send = lax.dynamic_index_in_dim(x, 1 - bit, axis, keepdims=False).astype(kind)
    return keep + partner(send, "tensor", distance).astype(jnp.float32)


def unfold(x, axis, distance):
    other = partner(x, "tensor", distance)
    upper = bit_of(distance) == 1
    return jnp.where(upper, jnp.stack([other, x], axis), jnp.stack([x, other], axis))


def depth_index():
    return lax.axis_index("tensor") >> DEEP


def depth_size():
    return lax.axis_size("tensor") >> DEEP


def across_depth(x, k):
    return lax.ppermute(x, "tensor", [(i, i ^ k << DEEP) for i in range(lax.axis_size("tensor"))])


def unfold_depth(x, axis):
    at = depth_index()
    got = [x] + [across_depth(x, k) for k in range(1, depth_size())]
    parts = []
    for place in range(depth_size()):
        part = got[-1]
        for k in range(depth_size() - 1):
            part = jnp.where(at ^ place == k, got[k], part)
        parts.append(part)
    return jnp.stack(parts, axis)


def depth_parts(x):
    at = depth_index()
    parts = [lax.dynamic_index_in_dim(x, at ^ k, 0, keepdims=False) for k in range(depth_size())]
    return parts[0], [part.astype(jnp.bfloat16) for part in parts[1:]]


def sent_down(sends):
    return [across_depth(send, k + 1) for k, send in enumerate(sends)]


def add_all(total, came):
    for part in came:
        total = total + part.astype(jnp.float32)
    return total


def sum_chips(first, second):
    first, second = lax.optimization_barrier((first, second))
    first = fold(first, 1, ACROSS)
    total, sends = depth_parts(first)
    second_total, second_sends = depth_parts(second)
    came, _ = lax.optimization_barrier((sent_down(second_sends), sends))
    second = fold(add_all(second_total, came), 0, ACROSS)
    return jnp.concatenate([add_all(total, sent_down(sends)), second], axis=-1)


def collect(rows, cut):
    first = unfold(unfold_depth(rows[:, :cut], 0), 1, ACROSS)
    second = unfold_depth(unfold(rows[:, cut:], 0, ACROSS), 0)
    both = unfold(jnp.concatenate([first, second], axis=-1), 2, CORE)
    return both.reshape(-1, both.shape[-1])


def local_pairs(
    tapped, join_weight, norm_gain, query_weight, kv_weight, out_weight, kv_cache, lengths, parents
):
    side = (lax.axis_index("tensor") % 2).astype(jnp.int32)
    row_count = tapped.shape[0]
    columns = join_weight.shape[1]
    sum_cut, cut = columns * 11 // 16, columns * 5 // 8
    spans = ((0, sum_cut), (sum_cut, columns))
    seq_count, piece_len = kv_cache.shape[:2]
    node_count = row_count // seq_count
    own_rows = row_count // 16
    row_ids = jnp.arange(row_count, dtype=jnp.int32)
    valid = jnp.clip(lengths - side * piece_len, 0, piece_len)
    info = jnp.concatenate([valid, side[None]]).astype(jnp.int32)
    parent_rows = row_ids // node_count * node_count + parents
    from_row = (parent_rows[:, :, None] == row_ids).astype(jnp.float32)
    hops = {}
    for step in range(STEPS):
        hops[step, step] = jnp.eye(row_count, dtype=jnp.float32)
        for earlier in range(step - 1, -1, -1):
            hops[step, earlier] = jnp.dot(hops[step, earlier + 1], from_row[earlier])
    bias = {at: (hop - 1.0) * -floor_score for at, hop in hops.items()}

    folded = []
    for start, end in spans:
        kept, sent = join(side, tapped, join_weight, start, end - start)
        part = kept + partner(sent, "tensor", CORE)
        folded.append(part.reshape(-1, 2, own_rows, end - start))
    hidden = sum_chips(*folded)

    keys, values = [], []
    for step in range(STEPS):
        normed = collect(normalize(hidden, norm_gain), cut)
        new_kv = jnp.dot(normed, kv_weight, preferred_element_type=jnp.float32)
        new_kv = new_kv.astype(jnp.bfloat16)
        query = jnp.dot(normed, query_weight, preferred_element_type=jnp.float32)
        query = query.astype(jnp.bfloat16)
        keys.append(partner(new_kv, "tensor", CORE))
        values.append(new_kv)
        kept, kept_lse, sent = attend(
            info, query, partner(query, "tensor", CORE), keys, values,
            [bias[step, t] for t in range(step + 1)], kv_cache,
        )
        came = partner(sent, "tensor", CORE)
        width = kept.shape[1]
        top = jnp.maximum(kept_lse, came[:, width:])
        mine = jnp.exp2(kept_lse - top)
        theirs = jnp.exp2(came[:, width:] - top)
        attended = (mine * kept + theirs * came[:, :width]) / (mine + theirs)
        update = jnp.dot(
            attended.astype(jnp.bfloat16), out_weight, preferred_element_type=jnp.float32
        ).reshape(-1, 2, 2, own_rows, columns)
        update = fold(update, 2, CORE)
        hidden = hidden + sum_chips(*[update[..., start:end] for start, end in spans])
    return hidden


def solution(mesh):
    body = local_pairs if mesh.shape["tensor"] == 2 * KVH else local_general
    placed = (
        P("groups", "tensor"),
        P("tensor", None),
        P(),
        P(None, "tensor"),
        P(None, "tensor"),
        P("tensor", None),
        P("groups", "tensor", None),
        P("groups"),
        P(None, "groups"),
    )
    return jax.shard_map(
        body, mesh=mesh, in_specs=placed, out_specs=P(("groups", "tensor"), None), check_vma=False
    )
```

profile of v0, /device:TPU:0, one launch (start us, length us, event | category | flops | bytes accessed | tf_op | source)
XLA Modules:
  0.0 295.5 jit_solution(12559842270123213843)
XLA Ops:
  1.3 13.1 %join.2 = (f32[64,5632]{1,0:T(8,128)S(1)}, f32[64,5632]{1,0:T(8,128)}) custom-call(s32[1]{0:T(128)} %bitcast.side_ref, bf16[128,3072]{1,0:T(8,128)(2,1)S(1)} %copy-done.1, bf16[3072,8192]{1,0:T(8,128)(2,1)} %weight_ref.3), custom_call_target="tpu_custom_call" | custom-call | flops 4429185024 | bytes 34603008 | tf_op jit(solution)/shard_map/join/pallas_call | solution.py:452
  14.9 7.7 %join.3 = (f32[64,2560]{1,0:T(8,128)S(1)}, f32[64,2560]{1,0:T(8,128)}) custom-call(s32[1]{0:T(128)} %bitcast.side_ref, bf16[128,3072]{1,0:T(8,128)(2,1)S(1)} %copy-done.1, bf16[3072,8192]{1,0:T(8,128)(2,1)} %weight_ref.3), custom_call_target="tpu_custom_call" | custom-call | flops 2013265920 | bytes 15728640 | tf_op jit(solution)/shard_map/join/pallas_call | solution.py:452
  23.5 2.4 collective-permute-done.1
  25.9 2.2 add.286
  30.8 2.7 collective-permute-start.2
  34.6 1.6 collective-permute-start.6
  36.2 2.6 collective-permute-start.7
  39.1 3.4 %collective-permute-done.2 = bf16[4,8,5632]{2,1,0:T(8,128)(2,1)S(1)} collective-permute-done((bf16[4,8,5632]{2,1,0:T(8,128)(2,1)S(1)}, bf16[4,8,5632]{2,1,0:T(8,128)(2,1)S(1)}, u32[]{:S(2)}, u32[]{:S(2)}) %collective-permute-start.2) | collective-permute-done | bytes 360480 | tf_op jit(solution)/shard_map/ppermute | solution.py:22
  43.7 2.0 collective-permute-done.7
  48.8 1.9 collective-permute-start.4
  52.2 5.5 %collective-permute-done.4 = bf16[8,5632]{1,0:T(8,128)(2,1)S(1)} collective-permute-done((bf16[8,5632]{1,0:T(8,128)(2,1)S(1)}, bf16[8,5632]{1,0:T(8,128)(2,1)S(1)}, u32[]{:S(2)}, u32[]{:S(2)}) %collective-permute-start.4) | collective-permute-done | bytes 90144 | tf_op jit(solution)/shard_map/ppermute | solution.py:505
  58.1 1.6 collective-permute-start.14
  59.7 1.9 collective-permute-start.10
  62.1 2.0 collective-permute-start.12
  66.5 2.2 collective-permute-done.10
  68.7 1.7 collective-permute-start.17
  71.4 4.7 %collective-permute-done.15 = bf16[2,8,3072]{2,1,0:T(8,128)(2,1)S(1)} collective-permute-done((bf16[2,8,3072]{2,1,0:T(8,128)(2,1)S(1)}, bf16[2,8,3072]{2,1,0:T(8,128)(2,1)S(1)}, u32[]{:S(2)}, u32[]{:S(2)}) %collective-permute-start.15) | collective-permute-done | bytes 98336 | tf_op jit(solution)/shard_map/ppermute | solution.py:505
  79.1 2.8 collective-permute-done.18
  82.0 1.8 maximum_select_fusion
  83.8 4.6 %convolution_convert_fusion.2.mine_ref = bf16[128,512]{1,0:T(8,128)(2,1)S(1)} fusion(bf16[128,8192]{1,0:T(8,128)(2,1)S(1)} %bitcast.265, bf16[8192,512]{1,0:T(8,128)(2,1)} %param.12), kind=kOutput, calls=%fused_computation.11 | convolution fusion | flops 1073807360 | bytes 10616832 | tf_op jit(solution)/shard_map/dot_general | solution.py:588
  90.6 15.6 %attend.3 = (f32[128,512]{1,0:T(8,128)S(1)}, f32[128,512]{1,0:T(8,128)S(1)}, f32[128,1024]{1,0:T(8,128)S(1)}) custom-call(s32[3]{0:T(128)S(1)} %pad_add_fusion.info_ref, bf16[128,512]{1,0:T(8,128)(2,1)S(1)} %convolution_convert_fusion.2.mine_ref, bf16[128,512]{1,0:T(8,128)(2,1)S(1)} %collective-permute-done.19.other_ref, ...), custom_call_target="tpu_custom_call" | custom-call | flops 8589934592 | bytes 16777216 | tf_op jit(solution)/shard_map/attend/pallas_call | solution.py:367
  106.3 2.0 collective-permute-done.21
  108.4 4.9 %fusion.50 = f32[128,8192]{1,0:T(8,128)S(1)} fusion(bf16[512,8192]{1,0:T(8,128)(2,1)} %param.14, f32[128,1024]{1,0:T(8,128)} %collective-permute-done.21, f32[128,512]{1,0:T(8,128)S(1)} %get-tuple-element.49, f32[128,512]{1,0:T(8,128)S(1)} %get-tuple-element.47), kind=kOutput, calls=%fused_computation.135 | convolution fusion | flops 1074462720 | bytes 13631488 | tf_op jit(solution)/shard_map/dot_general | solution.py:602
  113.3 2.0 copy-done.3
  115.6 2.7 collective-permute-done.22
  118.3 2.1 bitcast_add_fusion.2
  121.3 3.4 %collective-permute-start.27 = (bf16[2,8,2560]{2,1,0:T(8,128)(2,1)S(1)}, bf16[2,8,2560]{2,1,0:T(8,128)(2,1)S(1)}, u32[]{:S(2)}, u32[]{:S(2)}) collective-permute-start(bf16[2,8,2560]{2,1,0:T(8,128)(2,1)S(1)} %get-tuple-element.97), channel_id=1, source_target_pairs={{0,4},{1,5},{2,6},{3,7},{4,0},{5,1},{6,2},{7,3},{8,12},{9,13},{10,... | collective-permute-start | bytes 245768 | tf_op jit(solution)/shard_map/ppermute | solution.py:505
  125.3 1.9 collective-permute-start.29
  127.1 4.0 %collective-permute-done.23 = bf16[4,8,5632]{2,1,0:T(8,128)(2,1)S(1)} collective-permute-done((bf16[4,8,5632]{2,1,0:T(8,128)(2,1)S(1)}, bf16[4,8,5632]{2,1,0:T(8,128)(2,1)S(1)}, u32[]{:S(2)}, u32[]{:S(2)}) %collective-permute-start.23) | collective-permute-done | bytes 360480 | tf_op jit(solution)/shard_map/ppermute | solution.py:22
  131.3 2.5 collective-permute-done.28
  135.3 1.7 collective-permute-start.24
  137.8 1.9 collective-permute-start.26
  140.0 5.9 %collective-permute-done.25 = bf16[8,5632]{1,0:T(8,128)(2,1)S(1)} collective-permute-done((bf16[8,5632]{1,0:T(8,128)(2,1)S(1)}, bf16[8,5632]{1,0:T(8,128)(2,1)S(1)}, u32[]{:S(2)}, u32[]{:S(2)}) %collective-permute-start.25) | collective-permute-done | bytes 90144 | tf_op jit(solution)/shard_map/ppermute | solution.py:505
  147.0 2.1 collective-permute-start.31
  149.4 1.9 collective-permute-start.33
  153.9 1.6 collective-permute-done.31
  155.5 2.5 collective-permute-start.38
  159.6 4.1 %collective-permute-done.36 = bf16[2,8,3072]{2,1,0:T(8,128)(2,1)S(1)} collective-permute-done((bf16[2,8,3072]{2,1,0:T(8,128)(2,1)S(1)}, bf16[2,8,3072]{2,1,0:T(8,128)(2,1)S(1)}, u32[]{:S(2)}, u32[]{:S(2)}) %collective-permute-start.36) | collective-permute-done | bytes 98336 | tf_op jit(solution)/shard_map/ppermute | solution.py:505
  166.0 2.2 collective-permute-done.39
  172.3 16.3 %attend.4 = (f32[128,512]{1,0:T(8,128)S(1)}, f32[128,512]{1,0:T(8,128)S(1)}, f32[128,1024]{1,0:T(8,128)S(1)}) custom-call(s32[3]{0:T(128)S(1)} %pad_add_fusion.info_ref, bf16[128,512]{1,0:T(8,128)(2,1)S(1)} %convolution_convert_fusion.1.mine_ref, bf16[128,512]{1,0:T(8,128)(2,1)S(1)} %collective-permute-done.40.other_ref, ...), custom_call_target="tpu_custom_call" | custom-call | flops 8589934592 | bytes 16777216 | tf_op jit(solution)/shard_map/attend/pallas_call | solution.py:367
  188.7 1.9 collective-permute-done.42
  192.2 2.5 collective-permute-done.43
  196.7 3.6 %collective-permute-start.48 = (bf16[2,8,2560]{2,1,0:T(8,128)(2,1)S(1)}, bf16[2,8,2560]{2,1,0:T(8,128)(2,1)S(1)}, u32[]{:S(2)}, u32[]{:S(2)}) collective-permute-start(bf16[2,8,2560]{2,1,0:T(8,128)(2,1)S(1)} %get-tuple-element.94), channel_id=1, source_target_pairs={{0,4},{1,5},{2,6},{3,7},{4,0},{5,1},{6,2},{7,3},{8,12},{9,13},{10,... | collective-permute-start | bytes 245768 | tf_op jit(solution)/shard_map/ppermute | solution.py:505
  200.3 2.4 collective-permute-start.50
  202.7 3.0 %collective-permute-done.44 = bf16[4,8,5632]{2,1,0:T(8,128)(2,1)S(1)} collective-permute-done((bf16[4,8,5632]{2,1,0:T(8,128)(2,1)S(1)}, bf16[4,8,5632]{2,1,0:T(8,128)(2,1)S(1)}, u32[]{:S(2)}, u32[]{:S(2)}) %collective-permute-start.44) | collective-permute-done | bytes 360480 | tf_op jit(solution)/shard_map/ppermute | solution.py:22
  205.9 3.4 %collective-permute-done.49 = bf16[2,8,2560]{2,1,0:T(8,128)(2,1)S(1)} collective-permute-done((bf16[2,8,2560]{2,1,0:T(8,128)(2,1)S(1)}, bf16[2,8,2560]{2,1,0:T(8,128)(2,1)S(1)}, u32[]{:S(2)}, u32[]{:S(2)}) %collective-permute-start.49) | collective-permute-done | bytes 81952 | tf_op jit(solution)/shard_map/ppermute | solution.py:505
  209.8 1.6 collective-permute-start.45
  212.4 1.7 collective-permute-start.47
  214.7 5.7 %collective-permute-done.46 = bf16[8,5632]{1,0:T(8,128)(2,1)S(1)} collective-permute-done((bf16[8,5632]{1,0:T(8,128)(2,1)S(1)}, bf16[8,5632]{1,0:T(8,128)(2,1)S(1)}, u32[]{:S(2)}, u32[]{:S(2)}) %collective-permute-start.46) | collective-permute-done | bytes 90144 | tf_op jit(solution)/shard_map/ppermute | solution.py:505
  222.2 1.6 collective-permute-start.52
  224.3 2.3 collective-permute-start.54
  228.7 2.6 collective-permute-done.52
  234.1 5.0 %collective-permute-done.57 = bf16[2,8,3072]{2,1,0:T(8,128)(2,1)S(1)} collective-permute-done((bf16[2,8,3072]{2,1,0:T(8,128)(2,1)S(1)}, bf16[2,8,3072]{2,1,0:T(8,128)(2,1)S(1)}, u32[]{:S(2)}, u32[]{:S(2)}) %collective-permute-start.57) | collective-permute-done | bytes 98336 | tf_op jit(solution)/shard_map/ppermute | solution.py:505
  240.8 2.5 collective-permute-done.60
  247.3 15.7 %attend.5 = (f32[128,512]{1,0:T(8,128)S(1)}, f32[128,512]{1,0:T(8,128)S(1)}, f32[128,1024]{1,0:T(8,128)S(1)}) custom-call(s32[3]{0:T(128)S(1)} %pad_add_fusion.info_ref, bf16[128,512]{1,0:T(8,128)(2,1)S(1)} %convolution_convert_fusion.mine_ref, bf16[128,512]{1,0:T(8,128)(2,1)S(1)} %collective-permute-done.61.other_ref, ...), custom_call_target="tpu_custom_call" | custom-call | flops 8589934592 | bytes 16777216 | tf_op jit(solution)/shard_map/attend/pallas_call | solution.py:367
  263.1 1.9 collective-permute-done.63
  266.6 2.5 collective-permute-done.64
  270.6 3.1 %collective-permute-start.69 = (bf16[2,8,2560]{2,1,0:T(8,128)(2,1)S(1)}, bf16[2,8,2560]{2,1,0:T(8,128)(2,1)S(1)}, u32[]{:S(2)}, u32[]{:S(2)}) collective-permute-start(bf16[2,8,2560]{2,1,0:T(8,128)(2,1)S(1)} %get-tuple-element.91), channel_id=1, source_target_pairs={{0,4},{1,5},{2,6},{3,7},{4,0},{5,1},{6,2},{7,3},{8,12},{9,13},{10,... | collective-permute-start | bytes 245768 | tf_op jit(solution)/shard_map/ppermute | solution.py:505
  274.6 1.6 collective-permute-start.71
  276.2 4.0 %collective-permute-done.65 = bf16[4,8,5632]{2,1,0:T(8,128)(2,1)S(1)} collective-permute-done((bf16[4,8,5632]{2,1,0:T(8,128)(2,1)S(1)}, bf16[4,8,5632]{2,1,0:T(8,128)(2,1)S(1)}, u32[]{:S(2)}, u32[]{:S(2)}) %collective-permute-start.65) | collective-permute-done | bytes 360480 | tf_op jit(solution)/shard_map/ppermute | solution.py:22
  280.3 2.7 collective-permute-done.70
  284.4 1.6 collective-permute-start.66
  286.4 2.3 collective-permute-start.68
  288.9 5.8 %collective-permute-done.67 = bf16[8,5632]{1,0:T(8,128)(2,1)S(1)} collective-permute-done((bf16[8,5632]{1,0:T(8,128)(2,1)S(1)}, bf16[8,5632]{1,0:T(8,128)(2,1)S(1)}, u32[]{:S(2)}, u32[]{:S(2)}) %collective-permute-start.67) | collective-permute-done | bytes 90144 | tf_op jit(solution)/shard_map/ppermute | solution.py:505
  (220 shorter events, 63.9 us)
Async XLA Ops:
  14.4 13.7 %collective-permute-start = (f32[64,5632]{1,0:T(8,128)}, f32[64,5632]{1,0:T(8,128)}, u32[]{:S(2)}, u32[]{:S(2)}) collective-permute-start(f32[64,5632]{1,0:T(8,128)} %get-tuple-element.39), channel_id=1, source_target_pairs={{0,1},{1,0},{2,3},{3,2},{4,5},{5,4},{6,7},{7,6},{8,9},{9,8},{10,11... | collective-permute-start | bytes 4325384 | tf_op jit(solution)/shard_map/ppermute | solution.py:22
  23.5 2.4 collective-permute-start.1
  30.8 11.7 %collective-permute-start.2 = (bf16[4,8,5632]{2,1,0:T(8,128)(2,1)S(1)}, bf16[4,8,5632]{2,1,0:T(8,128)(2,1)S(1)}, u32[]{:S(2)}, u32[]{:S(2)}) collective-permute-start(bf16[4,8,5632]{2,1,0:T(8,128)(2,1)S(1)} %fusion.5), channel_id=1, source_target_pairs={{0,2},{1,3},{2,0},{3,1},{4,6},{5,7},{6,4},{7,5},{8,10},{9,11},{10,... | collective-permute-start | bytes 1081352 | tf_op jit(solution)/shard_map/ppermute | solution.py:22
  34.6 9.0 %collective-permute-start.6 = (bf16[2,8,2560]{2,1,0:T(8,128)(2,1)S(1)}, bf16[2,8,2560]{2,1,0:T(8,128)(2,1)S(1)}, u32[]{:S(2)}, u32[]{:S(2)}) collective-permute-start(bf16[2,8,2560]{2,1,0:T(8,128)(2,1)S(1)} %get-tuple-element.100), channel_id=1, source_target_pairs={{0,4},{1,5},{2,6},{3,7},{4,0},{5,1},{6,2},{7,3},{8,12},{9,13},{10,... | collective-permute-start | bytes 245768 | tf_op jit(solution)/shard_map/ppermute | solution.py:505
  36.2 9.4 %collective-permute-start.7 = (bf16[2,8,2560]{2,1,0:T(8,128)(2,1)S(1)}, bf16[2,8,2560]{2,1,0:T(8,128)(2,1)S(1)}, u32[]{:S(2)}, u32[]{:S(2)}) collective-permute-start(bf16[2,8,2560]{2,1,0:T(8,128)(2,1)S(1)} %get-tuple-element.99), channel_id=1, source_target_pairs={{0,8},{1,9},{2,10},{3,11},{4,12},{5,13},{6,14},{7,15},{8,0},{9,1},... | collective-permute-start | bytes 245768 | tf_op jit(solution)/shard_map/ppermute | solution.py:505
  38.8 6.8 %collective-permute-start.8 = (bf16[2,8,2560]{2,1,0:T(8,128)(2,1)S(1)}, bf16[2,8,2560]{2,1,0:T(8,128)(2,1)S(1)}, u32[]{:S(2)}, u32[]{:S(2)}) collective-permute-start(bf16[2,8,2560]{2,1,0:T(8,128)(2,1)S(1)} %get-tuple-element.98), channel_id=1, source_target_pairs={{0,12},{1,13},{2,14},{3,15},{4,8},{5,9},{6,10},{7,11},{8,4},{9,5},... | collective-permute-start | bytes 245768 | tf_op jit(solution)/shard_map/ppermute | solution.py:505
  46.7 5.0 %collective-permute-start.9 = (bf16[8,2560]{1,0:T(8,128)(2,1)S(1)}, bf16[8,2560]{1,0:T(8,128)(2,1)S(1)}, u32[]{:S(2)}, u32[]{:S(2)}) collective-permute-start(bf16[8,2560]{1,0:T(8,128)(2,1)S(1)} %fusion.80), channel_id=1, source_target_pairs={{0,2},{1,3},{2,0},{3,1},{4,6},{5,7},{6,4},{7,5},{8,10},{9,11},{10,... | collective-permute-start | bytes 122888 | tf_op jit(solution)/shard_map/ppermute | solution.py:22
  47.3 5.0 %collective-permute-start.3 = (bf16[8,5632]{1,0:T(8,128)(2,1)S(1)}, bf16[8,5632]{1,0:T(8,128)(2,1)S(1)}, u32[]{:S(2)}, u32[]{:S(2)}) collective-permute-start(bf16[8,5632]{1,0:T(8,128)(2,1)S(1)} %get-tuple-element.88), channel_id=1, source_target_pairs={{0,4},{1,5},{2,6},{3,7},{4,0},{5,1},{6,2},{7,3},{8,12},{9,13},{10,... | collective-permute-start | bytes 270344 | tf_op jit(solution)/shard_map/ppermute | solution.py:505
  48.8 9.0 %collective-permute-start.4 = (bf16[8,5632]{1,0:T(8,128)(2,1)S(1)}, bf16[8,5632]{1,0:T(8,128)(2,1)S(1)}, u32[]{:S(2)}, u32[]{:S(2)}) collective-permute-start(bf16[8,5632]{1,0:T(8,128)(2,1)S(1)} %get-tuple-element.87), channel_id=1, source_target_pairs={{0,8},{1,9},{2,10},{3,11},{4,12},{5,13},{6,14},{7,15},{8,0},{9,1},... | collective-permute-start | bytes 270344 | tf_op jit(solution)/shard_map/ppermute | solution.py:505
  50.6 7.1 %collective-permute-start.5 = (bf16[8,5632]{1,0:T(8,128)(2,1)S(1)}, bf16[8,5632]{1,0:T(8,128)(2,1)S(1)}, u32[]{:S(2)}, u32[]{:S(2)}) collective-permute-start(bf16[8,5632]{1,0:T(8,128)(2,1)S(1)} %get-tuple-element.86), channel_id=1, source_target_pairs={{0,12},{1,13},{2,14},{3,15},{4,8},{5,9},{6,10},{7,11},{8,4},{9,5},... | collective-permute-start | bytes 270344 | tf_op jit(solution)/shard_map/ppermute | solution.py:505
  58.1 6.0 %collective-permute-start.14 = (bf16[8,3072]{1,0:T(8,128)(2,1)S(1)}, bf16[8,3072]{1,0:T(8,128)(2,1)S(1)}, u32[]{:S(2)}, u32[]{:S(2)}) collective-permute-start(bf16[8,3072]{1,0:T(8,128)(2,1)S(1)} %get-tuple-element.135), channel_id=1, source_target_pairs={{0,2},{1,3},{2,0},{3,1},{4,6},{5,7},{6,4},{7,5},{8,10},{9,11},{10,... | collective-permute-start | bytes 147464 | tf_op jit(solution)/shard_map/ppermute | solution.py:22
  59.7 9.0 %collective-permute-start.10 = (bf16[8,5120]{1,0:T(8,128)(2,1)S(1)}, bf16[8,5120]{1,0:T(8,128)(2,1)S(1)}, u32[]{:S(2)}, u32[]{:S(2)}) collective-permute-start(bf16[8,5120]{1,0:T(8,128)(2,1)S(1)} %slice.84), channel_id=1, source_target_pairs={{0,8},{1,9},{2,10},{3,11},{4,12},{5,13},{6,14},{7,15},{8,0},{9,1},... | collective-permute-start | bytes 245768 | tf_op jit(solution)/shard_map/ppermute | solution.py:505
  61.6 8.9 %collective-permute-start.11 = (bf16[8,5120]{1,0:T(8,128)(2,1)S(1)}, bf16[8,5120]{1,0:T(8,128)(2,1)S(1)}, u32[]{:S(2)}, u32[]{:S(2)}) collective-permute-start(bf16[8,5120]{1,0:T(8,128)(2,1)S(1)} %slice.84), channel_id=1, source_target_pairs={{0,4},{1,5},{2,6},{3,7},{4,0},{5,1},{6,2},{7,3},{8,12},{9,13},{10,... | collective-permute-start | bytes 245768 | tf_op jit(solution)/shard_map/ppermute | solution.py:505
  62.1 8.5 %collective-permute-start.12 = (bf16[8,5120]{1,0:T(8,128)(2,1)S(1)}, bf16[8,5120]{1,0:T(8,128)(2,1)S(1)}, u32[]{:S(2)}, u32[]{:S(2)}) collective-permute-start(bf16[8,5120]{1,0:T(8,128)(2,1)S(1)} %slice.84), channel_id=1, source_target_pairs={{0,12},{1,13},{2,14},{3,15},{4,8},{5,9},{6,10},{7,11},{8,4},{9,5},... | collective-permute-start | bytes 245768 | tf_op jit(solution)/shard_map/ppermute | solution.py:505
  64.1 12.0 %collective-permute-start.15 = (bf16[2,8,3072]{2,1,0:T(8,128)(2,1)S(1)}, bf16[2,8,3072]{2,1,0:T(8,128)(2,1)S(1)}, u32[]{:S(2)}, u32[]{:S(2)}) collective-permute-start(bf16[2,8,3072]{2,1,0:T(8,128)(2,1)S(1)} %maximum_select_fusion.6), channel_id=1, source_target_pairs={{0,8},{1,9},{2,10},{3,11},{4,12},{5,13},{6,14},{7,15},{8,0},{9,1},... | collective-permute-start | bytes 294920 | tf_op jit(solution)/shard_map/ppermute | solution.py:505
  65.1 11.0 %collective-permute-start.16 = (bf16[2,8,3072]{2,1,0:T(8,128)(2,1)S(1)}, bf16[2,8,3072]{2,1,0:T(8,128)(2,1)S(1)}, u32[]{:S(2)}, u32[]{:S(2)}) collective-permute-start(bf16[2,8,3072]{2,1,0:T(8,128)(2,1)S(1)} %maximum_select_fusion.6), channel_id=1, source_target_pairs={{0,4},{1,5},{2,6},{3,7},{4,0},{5,1},{6,2},{7,3},{8,12},{9,13},{10,... | collective-permute-start | bytes 294920 | tf_op jit(solution)/shard_map/ppermute | solution.py:505
  68.7 7.4 %collective-permute-start.17 = (bf16[2,8,3072]{2,1,0:T(8,128)(2,1)S(1)}, bf16[2,8,3072]{2,1,0:T(8,128)(2,1)S(1)}, u32[]{:S(2)}, u32[]{:S(2)}) collective-permute-start(bf16[2,8,3072]{2,1,0:T(8,128)(2,1)S(1)} %maximum_select_fusion.6), channel_id=1, source_target_pairs={{0,12},{1,13},{2,14},{3,15},{4,8},{5,9},{6,10},{7,11},{8,4},{9,5},... | collective-permute-start | bytes 294920 | tf_op jit(solution)/shard_map/ppermute | solution.py:505
  70.7 7.1 %collective-permute-start.13 = (bf16[4,8,5120]{2,1,0:T(8,128)(2,1)S(1)}, bf16[4,8,5120]{2,1,0:T(8,128)(2,1)S(1)}, u32[]{:S(2)}, u32[]{:S(2)}) collective-permute-start(bf16[4,8,5120]{2,1,0:T(8,128)(2,1)S(1)} %get-tuple-element.129), channel_id=1, source_target_pairs={{0,2},{1,3},{2,0},{3,1},{4,6},{5,7},{6,4},{7,5},{8,10},{9,11},{10,... | collective-permute-start | bytes 983048 | tf_op jit(solution)/shard_map/ppermute | solution.py:22
  79.0 3.0 %collective-permute-start.18 = (bf16[4,2,8,8192]{3,2,1,0:T(8,128)(2,1)}, bf16[4,2,8,8192]{3,2,1,0:T(8,128)(2,1)}, u32[]{:S(2)}, u32[]{:S(2)}) collective-permute-start(bf16[4,2,8,8192]{3,2,1,0:T(8,128)(2,1)} %maximum_maximum_fusion), channel_id=1, source_target_pairs={{0,1},{1,0},{2,3},{3,2},{4,5},{5,4},{6,7},{7,6},{8,9},{9,8},{10,11... | collective-permute-start | bytes 3145736 | tf_op jit(solution)/shard_map/ppermute | solution.py:22
  115.4 2.9 collective-permute-start.22
  120.6 10.5 %collective-permute-start.23 = (bf16[4,8,5632]{2,1,0:T(8,128)(2,1)S(1)}, bf16[4,8,5632]{2,1,0:T(8,128)(2,1)S(1)}, u32[]{:S(2)}, u32[]{:S(2)}) collective-permute-start(bf16[4,8,5632]{2,1,0:T(8,128)(2,1)S(1)} %fusion.6), channel_id=1, source_target_pairs={{0,2},{1,3},{2,0},{3,1},{4,6},{5,7},{6,4},{7,5},{8,10},{9,11},{10,... | collective-permute-start | bytes 1081352 | tf_op jit(solution)/shard_map/ppermute | solution.py:22
  121.3 10.0 %collective-permute-start.27 = (bf16[2,8,2560]{2,1,0:T(8,128)(2,1)S(1)}, bf16[2,8,2560]{2,1,0:T(8,128)(2,1)S(1)}, u32[]{:S(2)}, u32[]{:S(2)}) collective-permute-start(bf16[2,8,2560]{2,1,0:T(8,128)(2,1)S(1)} %get-tuple-element.97), channel_id=1, source_target_pairs={{0,4},{1,5},{2,6},{3,7},{4,0},{5,1},{6,2},{7,3},{8,12},{9,13},{10,... | collective-permute-start | bytes 245768 | tf_op jit(solution)/shard_map/ppermute | solution.py:505
  124.7 9.1 %collective-permute-start.28 = (bf16[2,8,2560]{2,1,0:T(8,128)(2,1)S(1)}, bf16[2,8,2560]{2,1,0:T(8,128)(2,1)S(1)}, u32[]{:S(2)}, u32[]{:S(2)}) collective-permute-start(bf16[2,8,2560]{2,1,0:T(8,128)(2,1)S(1)} %get-tuple-element.96), channel_id=1, source_target_pairs={{0,8},{1,9},{2,10},{3,11},{4,12},{5,13},{6,14},{7,15},{8,0},{9,1},... | collective-permute-start | bytes 245768 | tf_op jit(solution)/shard_map/ppermute | solution.py:505
  125.3 8.5 %collective-permute-start.29 = (bf16[2,8,2560]{2,1,0:T(8,128)(2,1)S(1)}, bf16[2,8,2560]{2,1,0:T(8,128)(2,1)S(1)}, u32[]{:S(2)}, u32[]{:S(2)}) collective-permute-start(bf16[2,8,2560]{2,1,0:T(8,128)(2,1)S(1)} %get-tuple-element.95), channel_id=1, source_target_pairs={{0,12},{1,13},{2,14},{3,15},{4,8},{5,9},{6,10},{7,11},{8,4},{9,5},... | collective-permute-start | bytes 245768 | tf_op jit(solution)/shard_map/ppermute | solution.py:505
  133.8 5.9 %collective-permute-start.30 = (bf16[8,2560]{1,0:T(8,128)(2,1)S(1)}, bf16[8,2560]{1,0:T(8,128)(2,1)S(1)}, u32[]{:S(2)}, u32[]{:S(2)}) collective-permute-start(bf16[8,2560]{1,0:T(8,128)(2,1)S(1)} %fusion.81), channel_id=1, source_target_pairs={{0,2},{1,3},{2,0},{3,1},{4,6},{5,7},{6,4},{7,5},{8,10},{9,11},{10,... | collective-permute-start | bytes 122888 | tf_op jit(solution)/shard_map/ppermute | solution.py:22
  135.3 4.7 %collective-permute-start.24 = (bf16[8,5632]{1,0:T(8,128)(2,1)S(1)}, bf16[8,5632]{1,0:T(8,128)(2,1)S(1)}, u32[]{:S(2)}, u32[]{:S(2)}) collective-permute-start(bf16[8,5632]{1,0:T(8,128)(2,1)S(1)} %get-tuple-element.85), channel_id=1, source_target_pairs={{0,4},{1,5},{2,6},{3,7},{4,0},{5,1},{6,2},{7,3},{8,12},{9,13},{10,... | collective-permute-start | bytes 270344 | tf_op jit(solution)/shard_map/ppermute | solution.py:505
  137.0 8.9 %collective-permute-start.25 = (bf16[8,5632]{1,0:T(8,128)(2,1)S(1)}, bf16[8,5632]{1,0:T(8,128)(2,1)S(1)}, u32[]{:S(2)}, u32[]{:S(2)}) collective-permute-start(bf16[8,5632]{1,0:T(8,128)(2,1)S(1)} %get-tuple-element.84), channel_id=1, source_target_pairs={{0,8},{1,9},{2,10},{3,11},{4,12},{5,13},{6,14},{7,15},{8,0},{9,1},... | collective-permute-start | bytes 270344 | tf_op jit(solution)/shard_map/ppermute | solution.py:505
  137.8 8.1 %collective-permute-start.26 = (bf16[8,5632]{1,0:T(8,128)(2,1)S(1)}, bf16[8,5632]{1,0:T(8,128)(2,1)S(1)}, u32[]{:S(2)}, u32[]{:S(2)}) collective-permute-start(bf16[8,5632]{1,0:T(8,128)(2,1)S(1)} %get-tuple-element.83), channel_id=1, source_target_pairs={{0,12},{1,13},{2,14},{3,15},{4,8},{5,9},{6,10},{7,11},{8,4},{9,5},... | collective-permute-start | bytes 270344 | tf_op jit(solution)/shard_map/ppermute | solution.py:505
  146.2 5.1 %collective-permute-start.35 = (bf16[8,3072]{1,0:T(8,128)(2,1)S(1)}, bf16[8,3072]{1,0:T(8,128)(2,1)S(1)}, u32[]{:S(2)}, u32[]{:S(2)}) collective-permute-start(bf16[8,3072]{1,0:T(8,128)(2,1)S(1)} %get-tuple-element.133), channel_id=1, source_target_pairs={{0,2},{1,3},{2,0},{3,1},{4,6},{5,7},{6,4},{7,5},{8,10},{9,11},{10,... | collective-permute-start | bytes 147464 | tf_op jit(solution)/shard_map/ppermute | solution.py:22
  147.0 8.5 %collective-permute-start.31 = (bf16[8,5120]{1,0:T(8,128)(2,1)S(1)}, bf16[8,5120]{1,0:T(8,128)(2,1)S(1)}, u32[]{:S(2)}, u32[]{:S(2)}) collective-permute-start(bf16[8,5120]{1,0:T(8,128)(2,1)S(1)} %slice.90), channel_id=1, source_target_pairs={{0,8},{1,9},{2,10},{3,11},{4,12},{5,13},{6,14},{7,15},{8,0},{9,1},... | collective-permute-start | bytes 245768 | tf_op jit(solution)/shard_map/ppermute | solution.py:505
  149.1 8.9 %collective-permute-start.32 = (bf16[8,5120]{1,0:T(8,128)(2,1)S(1)}, bf16[8,5120]{1,0:T(8,128)(2,1)S(1)}, u32[]{:S(2)}, u32[]{:S(2)}) collective-permute-start(bf16[8,5120]{1,0:T(8,128)(2,1)S(1)} %slice.90), channel_id=1, source_target_pairs={{0,4},{1,5},{2,6},{3,7},{4,0},{5,1},{6,2},{7,3},{8,12},{9,13},{10,... | collective-permute-start | bytes 245768 | tf_op jit(solution)/shard_map/ppermute | solution.py:505
  149.4 8.6 %collective-permute-start.33 = (bf16[8,5120]{1,0:T(8,128)(2,1)S(1)}, bf16[8,5120]{1,0:T(8,128)(2,1)S(1)}, u32[]{:S(2)}, u32[]{:S(2)}) collective-permute-start(bf16[8,5120]{1,0:T(8,128)(2,1)S(1)} %slice.90), channel_id=1, source_target_pairs={{0,12},{1,13},{2,14},{3,15},{4,8},{5,9},{6,10},{7,11},{8,4},{9,5},... | collective-permute-start | bytes 245768 | tf_op jit(solution)/shard_map/ppermute | solution.py:505
  151.4 12.3 %collective-permute-start.36 = (bf16[2,8,3072]{2,1,0:T(8,128)(2,1)S(1)}, bf16[2,8,3072]{2,1,0:T(8,128)(2,1)S(1)}, u32[]{:S(2)}, u32[]{:S(2)}) collective-permute-start(bf16[2,8,3072]{2,1,0:T(8,128)(2,1)S(1)} %maximum_select_fusion.7), channel_id=1, source_target_pairs={{0,8},{1,9},{2,10},{3,11},{4,12},{5,13},{6,14},{7,15},{8,0},{9,1},... | collective-permute-start | bytes 294920 | tf_op jit(solution)/shard_map/ppermute | solution.py:505
  152.7 11.0 %collective-permute-start.37 = (bf16[2,8,3072]{2,1,0:T(8,128)(2,1)S(1)}, bf16[2,8,3072]{2,1,0:T(8,128)(2,1)S(1)}, u32[]{:S(2)}, u32[]{:S(2)}) collective-permute-start(bf16[2,8,3072]{2,1,0:T(8,128)(2,1)S(1)} %maximum_select_fusion.7), channel_id=1, source_target_pairs={{0,4},{1,5},{2,6},{3,7},{4,0},{5,1},{6,2},{7,3},{8,12},{9,13},{10,... | collective-permute-start | bytes 294920 | tf_op jit(solution)/shard_map/ppermute | solution.py:505
  155.5 8.2 %collective-permute-start.38 = (bf16[2,8,3072]{2,1,0:T(8,128)(2,1)S(1)}, bf16[2,8,3072]{2,1,0:T(8,128)(2,1)S(1)}, u32[]{:S(2)}, u32[]{:S(2)}) collective-permute-start(bf16[2,8,3072]{2,1,0:T(8,128)(2,1)S(1)} %maximum_select_fusion.7), channel_id=1, source_target_pairs={{0,12},{1,13},{2,14},{3,15},{4,8},{5,9},{6,10},{7,11},{8,4},{9,5},... | collective-permute-start | bytes 294920 | tf_op jit(solution)/shard_map/ppermute | solution.py:505
  158.1 7.1 %collective-permute-start.34 = (bf16[4,8,5120]{2,1,0:T(8,128)(2,1)S(1)}, bf16[4,8,5120]{2,1,0:T(8,128)(2,1)S(1)}, u32[]{:S(2)}, u32[]{:S(2)}) collective-permute-start(bf16[4,8,5120]{2,1,0:T(8,128)(2,1)S(1)} %get-tuple-element.127), channel_id=1, source_target_pairs={{0,2},{1,3},{2,0},{3,1},{4,6},{5,7},{6,4},{7,5},{8,10},{9,11},{10,... | collective-permute-start | bytes 983048 | tf_op jit(solution)/shard_map/ppermute | solution.py:22
  165.5 2.7 collective-permute-start.39
  192.0 2.7 collective-permute-start.43
  195.2 10.5 %collective-permute-start.44 = (bf16[4,8,5632]{2,1,0:T(8,128)(2,1)S(1)}, bf16[4,8,5632]{2,1,0:T(8,128)(2,1)S(1)}, u32[]{:S(2)}, u32[]{:S(2)}) collective-permute-start(bf16[4,8,5632]{2,1,0:T(8,128)(2,1)S(1)} %fusion.7), channel_id=1, source_target_pairs={{0,2},{1,3},{2,0},{3,1},{4,6},{5,7},{6,4},{7,5},{8,10},{9,11},{10,... | collective-permute-start | bytes 1081352 | tf_op jit(solution)/shard_map/ppermute | solution.py:22
  196.7 9.2 %collective-permute-start.48 = (bf16[2,8,2560]{2,1,0:T(8,128)(2,1)S(1)}, bf16[2,8,2560]{2,1,0:T(8,128)(2,1)S(1)}, u32[]{:S(2)}, u32[]{:S(2)}) collective-permute-start(bf16[2,8,2560]{2,1,0:T(8,128)(2,1)S(1)} %get-tuple-element.94), channel_id=1, source_target_pairs={{0,4},{1,5},{2,6},{3,7},{4,0},{5,1},{6,2},{7,3},{8,12},{9,13},{10,... | collective-permute-start | bytes 245768 | tf_op jit(solution)/shard_map/ppermute | solution.py:505
  200.3 9.0 %collective-permute-start.49 = (bf16[2,8,2560]{2,1,0:T(8,128)(2,1)S(1)}, bf16[2,8,2560]{2,1,0:T(8,128)(2,1)S(1)}, u32[]{:S(2)}, u32[]{:S(2)}) collective-permute-start(bf16[2,8,2560]{2,1,0:T(8,128)(2,1)S(1)} %get-tuple-element.93), channel_id=1, source_target_pairs={{0,8},{1,9},{2,10},{3,11},{4,12},{5,13},{6,14},{7,15},{8,0},{9,1},... | collective-permute-start | bytes 245768 | tf_op jit(solution)/shard_map/ppermute | solution.py:505
  200.3 9.0 %collective-permute-start.50 = (bf16[2,8,2560]{2,1,0:T(8,128)(2,1)S(1)}, bf16[2,8,2560]{2,1,0:T(8,128)(2,1)S(1)}, u32[]{:S(2)}, u32[]{:S(2)}) collective-permute-start(bf16[2,8,2560]{2,1,0:T(8,128)(2,1)S(1)} %get-tuple-element.92), channel_id=1, source_target_pairs={{0,12},{1,13},{2,14},{3,15},{4,8},{5,9},{6,10},{7,11},{8,4},{9,5},... | collective-permute-start | bytes 245768 | tf_op jit(solution)/shard_map/ppermute | solution.py:505
  209.4 4.8 %collective-permute-start.51 = (bf16[8,2560]{1,0:T(8,128)(2,1)S(1)}, bf16[8,2560]{1,0:T(8,128)(2,1)S(1)}, u32[]{:S(2)}, u32[]{:S(2)}) collective-permute-start(bf16[8,2560]{1,0:T(8,128)(2,1)S(1)} %fusion.82), channel_id=1, source_target_pairs={{0,2},{1,3},{2,0},{3,1},{4,6},{5,7},{6,4},{7,5},{8,10},{9,11},{10,... | collective-permute-start | bytes 122888 | tf_op jit(solution)/shard_map/ppermute | solution.py:22
  209.8 5.0 %collective-permute-start.45 = (bf16[8,5632]{1,0:T(8,128)(2,1)S(1)}, bf16[8,5632]{1,0:T(8,128)(2,1)S(1)}, u32[]{:S(2)}, u32[]{:S(2)}) collective-permute-start(bf16[8,5632]{1,0:T(8,128)(2,1)S(1)} %get-tuple-element.82), channel_id=1, source_target_pairs={{0,4},{1,5},{2,6},{3,7},{4,0},{5,1},{6,2},{7,3},{8,12},{9,13},{10,... | collective-permute-start | bytes 270344 | tf_op jit(solution)/shard_map/ppermute | solution.py:505
  211.4 9.0 %collective-permute-start.46 = (bf16[8,5632]{1,0:T(8,128)(2,1)S(1)}, bf16[8,5632]{1,0:T(8,128)(2,1)S(1)}, u32[]{:S(2)}, u32[]{:S(2)}) collective-permute-start(bf16[8,5632]{1,0:T(8,128)(2,1)S(1)} %get-tuple-element.81), channel_id=1, source_target_pairs={{0,8},{1,9},{2,10},{3,11},{4,12},{5,13},{6,14},{7,15},{8,0},{9,1},... | collective-permute-start | bytes 270344 | tf_op jit(solution)/shard_map/ppermute | solution.py:505
  212.4 8.0 %collective-permute-start.47 = (bf16[8,5632]{1,0:T(8,128)(2,1)S(1)}, bf16[8,5632]{1,0:T(8,128)(2,1)S(1)}, u32[]{:S(2)}, u32[]{:S(2)}) collective-permute-start(bf16[8,5632]{1,0:T(8,128)(2,1)S(1)} %get-tuple-element.80), channel_id=1, source_target_pairs={{0,12},{1,13},{2,14},{3,15},{4,8},{5,9},{6,10},{7,11},{8,4},{9,5},... | collective-permute-start | bytes 270344 | tf_op jit(solution)/shard_map/ppermute | solution.py:505
  220.8 5.8 %collective-permute-start.56 = (bf16[8,3072]{1,0:T(8,128)(2,1)S(1)}, bf16[8,3072]{1,0:T(8,128)(2,1)S(1)}, u32[]{:S(2)}, u32[]{:S(2)}) collective-permute-start(bf16[8,3072]{1,0:T(8,128)(2,1)S(1)} %get-tuple-element.131), channel_id=1, source_target_pairs={{0,2},{1,3},{2,0},{3,1},{4,6},{5,7},{6,4},{7,5},{8,10},{9,11},{10,... | collective-permute-start | bytes 147464 | tf_op jit(solution)/shard_map/ppermute | solution.py:22
  222.2 9.1 %collective-permute-start.52 = (bf16[8,5120]{1,0:T(8,128)(2,1)S(1)}, bf16[8,5120]{1,0:T(8,128)(2,1)S(1)}, u32[]{:S(2)}, u32[]{:S(2)}) collective-permute-start(bf16[8,5120]{1,0:T(8,128)(2,1)S(1)} %slice.97), channel_id=1, source_target_pairs={{0,8},{1,9},{2,10},{3,11},{4,12},{5,13},{6,14},{7,15},{8,0},{9,1},... | collective-permute-start | bytes 245768 | tf_op jit(solution)/shard_map/ppermute | solution.py:505
  223.8 8.0 %collective-permute-start.53 = (bf16[8,5120]{1,0:T(8,128)(2,1)S(1)}, bf16[8,5120]{1,0:T(8,128)(2,1)S(1)}, u32[]{:S(2)}, u32[]{:S(2)}) collective-permute-start(bf16[8,5120]{1,0:T(8,128)(2,1)S(1)} %slice.97), channel_id=1, source_target_pairs={{0,4},{1,5},{2,6},{3,7},{4,0},{5,1},{6,2},{7,3},{8,12},{9,13},{10,... | collective-permute-start | bytes 245768 | tf_op jit(solution)/shard_map/ppermute | solution.py:505
  224.3 8.8 %collective-permute-start.54 = (bf16[8,5120]{1,0:T(8,128)(2,1)S(1)}, bf16[8,5120]{1,0:T(8,128)(2,1)S(1)}, u32[]{:S(2)}, u32[]{:S(2)}) collective-permute-start(bf16[8,5120]{1,0:T(8,128)(2,1)S(1)} %slice.97), channel_id=1, source_target_pairs={{0,12},{1,13},{2,14},{3,15},{4,8},{5,9},{6,10},{7,11},{8,4},{9,5},... | collective-permute-start | bytes 245768 | tf_op jit(solution)/shard_map/ppermute | solution.py:505
  226.6 12.5 %collective-permute-start.57 = (bf16[2,8,3072]{2,1,0:T(8,128)(2,1)S(1)}, bf16[2,8,3072]{2,1,0:T(8,128)(2,1)S(1)}, u32[]{:S(2)}, u32[]{:S(2)}) collective-permute-start(bf16[2,8,3072]{2,1,0:T(8,128)(2,1)S(1)} %maximum_select_fusion.8), channel_id=1, source_target_pairs={{0,8},{1,9},{2,10},{3,11},{4,12},{5,13},{6,14},{7,15},{8,0},{9,1},... | collective-permute-start | bytes 294920 | tf_op jit(solution)/shard_map/ppermute | solution.py:505
  227.3 11.8 %collective-permute-start.58 = (bf16[2,8,3072]{2,1,0:T(8,128)(2,1)S(1)}, bf16[2,8,3072]{2,1,0:T(8,128)(2,1)S(1)}, u32[]{:S(2)}, u32[]{:S(2)}) collective-permute-start(bf16[2,8,3072]{2,1,0:T(8,128)(2,1)S(1)} %maximum_select_fusion.8), channel_id=1, source_target_pairs={{0,4},{1,5},{2,6},{3,7},{4,0},{5,1},{6,2},{7,3},{8,12},{9,13},{10,... | collective-permute-start | bytes 294920 | tf_op jit(solution)/shard_map/ppermute | solution.py:505
  231.3 7.8 %collective-permute-start.59 = (bf16[2,8,3072]{2,1,0:T(8,128)(2,1)S(1)}, bf16[2,8,3072]{2,1,0:T(8,128)(2,1)S(1)}, u32[]{:S(2)}, u32[]{:S(2)}) collective-permute-start(bf16[2,8,3072]{2,1,0:T(8,128)(2,1)S(1)} %maximum_select_fusion.8), channel_id=1, source_target_pairs={{0,12},{1,13},{2,14},{3,15},{4,8},{5,9},{6,10},{7,11},{8,4},{9,5},... | collective-permute-start | bytes 294920 | tf_op jit(solution)/shard_map/ppermute | solution.py:505
  233.1 7.1 %collective-permute-start.55 = (bf16[4,8,5120]{2,1,0:T(8,128)(2,1)S(1)}, bf16[4,8,5120]{2,1,0:T(8,128)(2,1)S(1)}, u32[]{:S(2)}, u32[]{:S(2)}) collective-permute-start(bf16[4,8,5120]{2,1,0:T(8,128)(2,1)S(1)} %get-tuple-element.125), channel_id=1, source_target_pairs={{0,2},{1,3},{2,0},{3,1},{4,6},{5,7},{6,4},{7,5},{8,10},{9,11},{10,... | collective-permute-start | bytes 983048 | tf_op jit(solution)/shard_map/ppermute | solution.py:22
  240.6 2.7 collective-permute-start.60
  266.4 2.7 collective-permute-start.64
  269.6 10.5 %collective-permute-start.65 = (bf16[4,8,5632]{2,1,0:T(8,128)(2,1)S(1)}, bf16[4,8,5632]{2,1,0:T(8,128)(2,1)S(1)}, u32[]{:S(2)}, u32[]{:S(2)}) collective-permute-start(bf16[4,8,5632]{2,1,0:T(8,128)(2,1)S(1)} %fusion.8), channel_id=1, source_target_pairs={{0,2},{1,3},{2,0},{3,1},{4,6},{5,7},{6,4},{7,5},{8,10},{9,11},{10,... | collective-permute-start | bytes 1081352 | tf_op jit(solution)/shard_map/ppermute | solution.py:22
  270.6 9.6 %collective-permute-start.69 = (bf16[2,8,2560]{2,1,0:T(8,128)(2,1)S(1)}, bf16[2,8,2560]{2,1,0:T(8,128)(2,1)S(1)}, u32[]{:S(2)}, u32[]{:S(2)}) collective-permute-start(bf16[2,8,2560]{2,1,0:T(8,128)(2,1)S(1)} %get-tuple-element.91), channel_id=1, source_target_pairs={{0,4},{1,5},{2,6},{3,7},{4,0},{5,1},{6,2},{7,3},{8,12},{9,13},{10,... | collective-permute-start | bytes 245768 | tf_op jit(solution)/shard_map/ppermute | solution.py:505
  273.7 9.2 %collective-permute-start.70 = (bf16[2,8,2560]{2,1,0:T(8,128)(2,1)S(1)}, bf16[2,8,2560]{2,1,0:T(8,128)(2,1)S(1)}, u32[]{:S(2)}, u32[]{:S(2)}) collective-permute-start(bf16[2,8,2560]{2,1,0:T(8,128)(2,1)S(1)} %get-tuple-element.90), channel_id=1, source_target_pairs={{0,8},{1,9},{2,10},{3,11},{4,12},{5,13},{6,14},{7,15},{8,0},{9,1},... | collective-permute-start | bytes 245768 | tf_op jit(solution)/shard_map/ppermute | solution.py:505
  274.6 8.3 %collective-permute-start.71 = (bf16[2,8,2560]{2,1,0:T(8,128)(2,1)S(1)}, bf16[2,8,2560]{2,1,0:T(8,128)(2,1)S(1)}, u32[]{:S(2)}, u32[]{:S(2)}) collective-permute-start(bf16[2,8,2560]{2,1,0:T(8,128)(2,1)S(1)} %get-tuple-element.89), channel_id=1, source_target_pairs={{0,12},{1,13},{2,14},{3,15},{4,8},{5,9},{6,10},{7,11},{8,4},{9,5},... | collective-permute-start | bytes 245768 | tf_op jit(solution)/shard_map/ppermute | solution.py:505
  283.0 5.7 %collective-permute-start.72 = (bf16[8,2560]{1,0:T(8,128)(2,1)S(1)}, bf16[8,2560]{1,0:T(8,128)(2,1)S(1)}, u32[]{:S(2)}, u32[]{:S(2)}) collective-permute-start(bf16[8,2560]{1,0:T(8,128)(2,1)S(1)} %fusion.83), channel_id=1, source_target_pairs={{0,2},{1,3},{2,0},{3,1},{4,6},{5,7},{6,4},{7,5},{8,10},{9,11},{10,... | collective-permute-start | bytes 122888 | tf_op jit(solution)/shard_map/ppermute | solution.py:22
  284.4 4.6 %collective-permute-start.66 = (bf16[8,5632]{1,0:T(8,128)(2,1)S(1)}, bf16[8,5632]{1,0:T(8,128)(2,1)S(1)}, u32[]{:S(2)}, u32[]{:S(2)}) collective-permute-start(bf16[8,5632]{1,0:T(8,128)(2,1)S(1)} %get-tuple-element.79), channel_id=1, source_target_pairs={{0,4},{1,5},{2,6},{3,7},{4,0},{5,1},{6,2},{7,3},{8,12},{9,13},{10,... | collective-permute-start | bytes 270344 | tf_op jit(solution)/shard_map/ppermute | solution.py:505
  286.0 8.7 %collective-permute-start.67 = (bf16[8,5632]{1,0:T(8,128)(2,1)S(1)}, bf16[8,5632]{1,0:T(8,128)(2,1)S(1)}, u32[]{:S(2)}, u32[]{:S(2)}) collective-permute-start(bf16[8,5632]{1,0:T(8,128)(2,1)S(1)} %get-tuple-element.78), channel_id=1, source_target_pairs={{0,8},{1,9},{2,10},{3,11},{4,12},{5,13},{6,14},{7,15},{8,0},{9,1},... | collective-permute-start | bytes 270344 | tf_op jit(solution)/shard_map/ppermute | solution.py:505
  286.4 8.3 %collective-permute-start.68 = (bf16[8,5632]{1,0:T(8,128)(2,1)S(1)}, bf16[8,5632]{1,0:T(8,128)(2,1)S(1)}, u32[]{:S(2)}, u32[]{:S(2)}) collective-permute-start(bf16[8,5632]{1,0:T(8,128)(2,1)S(1)} %get-tuple-element.77), channel_id=1, source_target_pairs={{0,12},{1,13},{2,14},{3,15},{4,8},{5,9},{6,10},{7,11},{8,4},{9,5},... | collective-permute-start | bytes 270344 | tf_op jit(solution)/shard_map/ppermute | solution.py:505
  (23 other events, 233.3 us)
where the time goes:
time: 296 us
  waiting for transfers between devices  100 us (34%)
  starting transfers between devices  84.1 us (28%)
  Pallas kernels  68.4 us (23%)
  matrix products  17.3 us (6%)
  other arithmetic  16.4 us (6%)
  local copies, waits for them, and re-layouts  8.38 us (3%)
    ppermute x42, starting transfers between devices, across_depth(): lax.ppermute(x, 'tensor', [(i, i ^ k << DEEP) for i in range(lax.axis_siz...  64.4 us
    ppermute x42, waiting for transfers between devices, across_depth(): lax.ppermute(x, 'tensor', [(i, i ^ k << DEEP) for i in range(lax.axis_siz...  56.6 us
    pallas_call x3, Pallas kernels, attend(): pl.pallas_call(functools.partial(attend_kernel, depth), out_shape=(jax.Sh...  47.6 us
    ppermute x31, waiting for transfers between devices, partner(): lax.ppermute(x, axis, [(i, i ^ 1 << distance) for i in range(lax.axis_siz...  43.5 us
    pallas_call x2, Pallas kernels, join(): pl.pallas_call(functools.partial(join_kernel, start), out_shape=(out, out...  20.8 us
    ppermute x31, starting transfers between devices, partner(): lax.ppermute(x, axis, [(i, i ^ 1 << distance) for i in range(lax.axis_siz...  19.7 us
    dot_general x3, matrix products, local_pairs(): jnp.dot(attended.astype(jnp.bfloat16), out_weight, preferred_element_type...  7.62 us
    dot_general x3, matrix products, local_pairs(): query = jnp.dot(normed, query_weight, preferred_element_type=jnp.float32)  7.15 us
  transfers between devices with their start and end apart: 73, of which 40 were waited for; matrix products, arithmetic and copies ran while one was open for 3% of the time, Pallas kernels for 3%

commit v1 on v0

--- a/solution.py
+++ b/solution.py
@@ -387,7 +387,7 @@
             pltpu.VMEM((2, BLOCK, HD), jnp.bfloat16),
             pltpu.SemaphoreType.DMA((3,)),
         ],
-        compiler_params=pltpu.CompilerParams(vmem_limit_bytes=24 * 1024 * 1024),
+        compiler_params=pltpu.CompilerParams(vmem_limit_bytes=18 * 1024 * 1024),
         cost_estimate=pl.CostEstimate(
             flops=4 * all_rows * slot_count * HD,
             bytes_accessed=2 * cache.size,
@@ -401,7 +401,7 @@
 
 
 STRIP = 256
-STRIPS = 4
+STRIPS = 3
 TILE = 512
 
 
@@ -465,7 +465,7 @@
             pltpu.SemaphoreType.DMA,
             pltpu.SemaphoreType.DMA((STRIPS,)),
         ],
-        compiler_params=pltpu.CompilerParams(vmem_limit_bytes=32 * 1024 * 1024),
+        compiler_params=pltpu.CompilerParams(vmem_limit_bytes=20 * 1024 * 1024),
         cost_estimate=pl.CostEstimate(
             flops=2 * rows * depth * columns, bytes_accessed=2 * depth * columns, transcendentals=0
         ),

time: 296 us -> 298 us (level)
  no operation moved by 1% of the time
where the time goes in v1:
time: 298 us
  waiting for transfers between devices  100 us (34%)
  starting transfers between devices  84.1 us (28%)
  Pallas kernels  70.1 us (24%)
  matrix products  17.7 us (6%)
  other arithmetic  16.5 us (6%)
  local copies, waits for them, and re-layouts  8.3 us (3%)
    ppermute x42, starting transfers between devices, across_depth(): lax.ppermute(x, 'tensor', [(i, i ^ k << DEEP) for i in range(lax.axis_siz...  64.3 us
    ppermute x42, waiting for transfers between devices, across_depth(): lax.ppermute(x, 'tensor', [(i, i ^ k << DEEP) for i in range(lax.axis_siz...  56.7 us
    pallas_call x3, Pallas kernels, attend(): pl.pallas_call(functools.partial(attend_kernel, depth), out_shape=(jax.Sh...  47.6 us
    ppermute x31, waiting for transfers between devices, partner(): lax.ppermute(x, axis, [(i, i ^ 1 << distance) for i in range(lax.axis_siz...  43.5 us
    pallas_call x2, Pallas kernels, join(): pl.pallas_call(functools.partial(join_kernel, start), out_shape=(out, out...  22.5 us
    ppermute x31, starting transfers between devices, partner(): lax.ppermute(x, axis, [(i, i ^ 1 << distance) for i in range(lax.axis_siz...  19.8 us
    dot_general x3, matrix products, local_pairs(): jnp.dot(attended.astype(jnp.bfloat16), out_weight, preferred_element_type...  7.65 us
    dot_general x3, matrix products, local_pairs(): query = jnp.dot(normed, query_weight, preferred_element_type=jnp.float32)  7.4 us
  transfers between devices with their start and end apart: 73, of which 40 were waited for; matrix products, arithmetic and copies ran while one was open for 3% of the time, Pallas kernels for 3%

profile of v1, /device:TPU:0, one launch (start us, length us, event | category | flops | bytes accessed | tf_op | source)
XLA Modules:
  0.0 297.6 jit_solution(12402478047507622576)
XLA Ops:
  1.3 13.4 %join.2 = (f32[64,5632]{1,0:T(8,128)S(1)}, f32[64,5632]{1,0:T(8,128)}) custom-call(s32[1]{0:T(128)} %bitcast.side_ref, bf16[128,3072]{1,0:T(8,128)(2,1)S(1)} %copy-done.1, bf16[3072,8192]{1,0:T(8,128)(2,1)} %weight_ref.3), custom_call_target="tpu_custom_call" | custom-call | flops 4429185024 | bytes 34603008 | tf_op jit(solution)/shard_map/join/pallas_call | solution.py:452
  15.2 9.0 %join.3 = (f32[64,2560]{1,0:T(8,128)S(1)}, f32[64,2560]{1,0:T(8,128)}) custom-call(s32[1]{0:T(128)} %bitcast.side_ref, bf16[128,3072]{1,0:T(8,128)(2,1)S(1)} %copy-done.1, bf16[3072,8192]{1,0:T(8,128)(2,1)} %weight_ref.3), custom_call_target="tpu_custom_call" | custom-call | flops 2013265920 | bytes 15728640 | tf_op jit(solution)/shard_map/join/pallas_call | solution.py:452
  25.2 2.4 collective-permute-done.1
  27.6 2.2 add.286
  32.5 2.7 collective-permute-start.2
  36.3 1.7 collective-permute-start.6
  37.9 2.6 collective-permute-start.7
  40.7 3.4 %collective-permute-done.2 = bf16[4,8,5632]{2,1,0:T(8,128)(2,1)S(1)} collective-permute-done((bf16[4,8,5632]{2,1,0:T(8,128)(2,1)S(1)}, bf16[4,8,5632]{2,1,0:T(8,128)(2,1)S(1)}, u32[]{:S(2)}, u32[]{:S(2)}) %collective-permute-start.2) | collective-permute-done | bytes 360480 | tf_op jit(solution)/shard_map/ppermute | solution.py:22
  45.3 2.0 collective-permute-done.7
  50.4 1.9 collective-permute-start.4
  53.9 5.5 %collective-permute-done.4 = bf16[8,5632]{1,0:T(8,128)(2,1)S(1)} collective-permute-done((bf16[8,5632]{1,0:T(8,128)(2,1)S(1)}, bf16[8,5632]{1,0:T(8,128)(2,1)S(1)}, u32[]{:S(2)}, u32[]{:S(2)}) %collective-permute-start.4) | collective-permute-done | bytes 90144 | tf_op jit(solution)/shard_map/ppermute | solution.py:505
  59.8 1.6 collective-permute-start.14
  61.4 1.9 collective-permute-start.10
  63.8 2.0 collective-permute-start.12
  68.2 2.1 collective-permute-done.10
  70.4 1.8 collective-permute-start.17
  73.0 4.7 %collective-permute-done.15 = bf16[2,8,3072]{2,1,0:T(8,128)(2,1)S(1)} collective-permute-done((bf16[2,8,3072]{2,1,0:T(8,128)(2,1)S(1)}, bf16[2,8,3072]{2,1,0:T(8,128)(2,1)S(1)}, u32[]{:S(2)}, u32[]{:S(2)}) %collective-permute-start.15) | collective-permute-done | bytes 98336 | tf_op jit(solution)/shard_map/ppermute | solution.py:505
  80.8 2.8 collective-permute-done.18
  83.6 1.8 maximum_select_fusion
  85.4 4.6 %convolution_convert_fusion.2.mine_ref = bf16[128,512]{1,0:T(8,128)(2,1)S(1)} fusion(bf16[128,8192]{1,0:T(8,128)(2,1)S(1)} %bitcast.265, bf16[8192,512]{1,0:T(8,128)(2,1)} %param.12), kind=kOutput, calls=%fused_computation.11 | convolution fusion | flops 1073807360 | bytes 10616832 | tf_op jit(solution)/shard_map/dot_general | solution.py:588
  92.3 15.6 %attend.3 = (f32[128,512]{1,0:T(8,128)S(1)}, f32[128,512]{1,0:T(8,128)S(1)}, f32[128,1024]{1,0:T(8,128)S(1)}) custom-call(s32[3]{0:T(128)S(1)} %pad_add_fusion.info_ref, bf16[128,512]{1,0:T(8,128)(2,1)S(1)} %convolution_convert_fusion.2.mine_ref, bf16[128,512]{1,0:T(8,128)(2,1)S(1)} %collective-permute-done.19.other_ref, ...), custom_call_target="tpu_custom_call" | custom-call | flops 8589934592 | bytes 16777216 | tf_op jit(solution)/shard_map/attend/pallas_call | solution.py:367
  108.0 2.0 collective-permute-done.21
  110.0 4.9 %fusion.50 = f32[128,8192]{1,0:T(8,128)S(1)} fusion(bf16[512,8192]{1,0:T(8,128)(2,1)} %param.14, f32[128,1024]{1,0:T(8,128)} %collective-permute-done.21, f32[128,512]{1,0:T(8,128)S(1)} %get-tuple-element.49, f32[128,512]{1,0:T(8,128)S(1)} %get-tuple-element.47), kind=kOutput, calls=%fused_computation.135 | convolution fusion | flops 1074462720 | bytes 13631488 | tf_op jit(solution)/shard_map/dot_general | solution.py:602
  115.0 2.0 copy-done.3
  117.3 2.7 collective-permute-done.22
  120.0 2.1 bitcast_add_fusion.2
  123.0 3.4 %collective-permute-start.27 = (bf16[2,8,2560]{2,1,0:T(8,128)(2,1)S(1)}, bf16[2,8,2560]{2,1,0:T(8,128)(2,1)S(1)}, u32[]{:S(2)}, u32[]{:S(2)}) collective-permute-start(bf16[2,8,2560]{2,1,0:T(8,128)(2,1)S(1)} %get-tuple-element.97), channel_id=1, source_target_pairs={{0,4},{1,5},{2,6},{3,7},{4,0},{5,1},{6,2},{7,3},{8,12},{9,13},{10,... | collective-permute-start | bytes 245768 | tf_op jit(solution)/shard_map/ppermute | solution.py:505
  126.9 1.9 collective-permute-start.29
  128.8 4.0 %collective-permute-done.23 = bf16[4,8,5632]{2,1,0:T(8,128)(2,1)S(1)} collective-permute-done((bf16[4,8,5632]{2,1,0:T(8,128)(2,1)S(1)}, bf16[4,8,5632]{2,1,0:T(8,128)(2,1)S(1)}, u32[]{:S(2)}, u32[]{:S(2)}) %collective-permute-start.23) | collective-permute-done | bytes 360480 | tf_op jit(solution)/shard_map/ppermute | solution.py:22
  132.9 2.5 collective-permute-done.28
  137.0 1.7 collective-permute-start.24
  139.5 1.9 collective-permute-start.26
  141.6 5.9 %collective-permute-done.25 = bf16[8,5632]{1,0:T(8,128)(2,1)S(1)} collective-permute-done((bf16[8,5632]{1,0:T(8,128)(2,1)S(1)}, bf16[8,5632]{1,0:T(8,128)(2,1)S(1)}, u32[]{:S(2)}, u32[]{:S(2)}) %collective-permute-start.25) | collective-permute-done | bytes 90144 | tf_op jit(solution)/shard_map/ppermute | solution.py:505
  148.6 2.1 collective-permute-start.31
  151.1 1.9 collective-permute-start.33
  155.6 1.7 collective-permute-done.31
  157.2 2.4 collective-permute-start.38
  161.3 4.1 %collective-permute-done.36 = bf16[2,8,3072]{2,1,0:T(8,128)(2,1)S(1)} collective-permute-done((bf16[2,8,3072]{2,1,0:T(8,128)(2,1)S(1)}, bf16[2,8,3072]{2,1,0:T(8,128)(2,1)S(1)}, u32[]{:S(2)}, u32[]{:S(2)}) %collective-permute-start.36) | collective-permute-done | bytes 98336 | tf_op jit(solution)/shard_map/ppermute | solution.py:505
  167.7 2.3 collective-permute-done.39
  174.1 16.3 %attend.4 = (f32[128,512]{1,0:T(8,128)S(1)}, f32[128,512]{1,0:T(8,128)S(1)}, f32[128,1024]{1,0:T(8,128)S(1)}) custom-call(s32[3]{0:T(128)S(1)} %pad_add_fusion.info_ref, bf16[128,512]{1,0:T(8,128)(2,1)S(1)} %convolution_convert_fusion.1.mine_ref, bf16[128,512]{1,0:T(8,128)(2,1)S(1)} %collective-permute-done.40.other_ref, ...), custom_call_target="tpu_custom_call" | custom-call | flops 8589934592 | bytes 16777216 | tf_op jit(solution)/shard_map/attend/pallas_call | solution.py:367
  190.5 1.9 collective-permute-done.42
  194.1 2.5 collective-permute-done.43
  198.6 3.6 %collective-permute-start.48 = (bf16[2,8,2560]{2,1,0:T(8,128)(2,1)S(1)}, bf16[2,8,2560]{2,1,0:T(8,128)(2,1)S(1)}, u32[]{:S(2)}, u32[]{:S(2)}) collective-permute-start(bf16[2,8,2560]{2,1,0:T(8,128)(2,1)S(1)} %get-tuple-element.94), channel_id=1, source_target_pairs={{0,4},{1,5},{2,6},{3,7},{4,0},{5,1},{6,2},{7,3},{8,12},{9,13},{10,... | collective-permute-start | bytes 245768 | tf_op jit(solution)/shard_map/ppermute | solution.py:505
  202.2 2.4 collective-permute-start.50
  204.6 2.9 collective-permute-done.44
  207.7 3.5 %collective-permute-done.49 = bf16[2,8,2560]{2,1,0:T(8,128)(2,1)S(1)} collective-permute-done((bf16[2,8,2560]{2,1,0:T(8,128)(2,1)S(1)}, bf16[2,8,2560]{2,1,0:T(8,128)(2,1)S(1)}, u32[]{:S(2)}, u32[]{:S(2)}) %collective-permute-start.49) | collective-permute-done | bytes 81952 | tf_op jit(solution)/shard_map/ppermute | solution.py:505
  211.7 1.6 collective-permute-start.45
  214.3 1.7 collective-permute-start.47
  216.6 5.7 %collective-permute-done.46 = bf16[8,5632]{1,0:T(8,128)(2,1)S(1)} collective-permute-done((bf16[8,5632]{1,0:T(8,128)(2,1)S(1)}, bf16[8,5632]{1,0:T(8,128)(2,1)S(1)}, u32[]{:S(2)}, u32[]{:S(2)}) %collective-permute-start.46) | collective-permute-done | bytes 90144 | tf_op jit(solution)/shard_map/ppermute | solution.py:505
  224.1 1.6 collective-permute-start.52
  226.1 2.3 collective-permute-start.54
  230.6 2.6 collective-permute-done.52
  236.0 5.0 %collective-permute-done.57 = bf16[2,8,3072]{2,1,0:T(8,128)(2,1)S(1)} collective-permute-done((bf16[2,8,3072]{2,1,0:T(8,128)(2,1)S(1)}, bf16[2,8,3072]{2,1,0:T(8,128)(2,1)S(1)}, u32[]{:S(2)}, u32[]{:S(2)}) %collective-permute-start.57) | collective-permute-done | bytes 98336 | tf_op jit(solution)/shard_map/ppermute | solution.py:505
  242.7 2.5 collective-permute-done.60
  249.4 15.7 %attend.5 = (f32[128,512]{1,0:T(8,128)S(1)}, f32[128,512]{1,0:T(8,128)S(1)}, f32[128,1024]{1,0:T(8,128)S(1)}) custom-call(s32[3]{0:T(128)S(1)} %pad_add_fusion.info_ref, bf16[128,512]{1,0:T(8,128)(2,1)S(1)} %convolution_convert_fusion.mine_ref, bf16[128,512]{1,0:T(8,128)(2,1)S(1)} %collective-permute-done.61.other_ref, ...), custom_call_target="tpu_custom_call" | custom-call | flops 8589934592 | bytes 16777216 | tf_op jit(solution)/shard_map/attend/pallas_call | solution.py:367
  265.1 1.9 collective-permute-done.63
  268.7 2.5 collective-permute-done.64
  272.7 3.1 %collective-permute-start.69 = (bf16[2,8,2560]{2,1,0:T(8,128)(2,1)S(1)}, bf16[2,8,2560]{2,1,0:T(8,128)(2,1)S(1)}, u32[]{:S(2)}, u32[]{:S(2)}) collective-permute-start(bf16[2,8,2560]{2,1,0:T(8,128)(2,1)S(1)} %get-tuple-element.91), channel_id=1, source_target_pairs={{0,4},{1,5},{2,6},{3,7},{4,0},{5,1},{6,2},{7,3},{8,12},{9,13},{10,... | collective-permute-start | bytes 245768 | tf_op jit(solution)/shard_map/ppermute | solution.py:505
  276.7 1.5 collective-permute-start.71
  278.3 4.0 %collective-permute-done.65 = bf16[4,8,5632]{2,1,0:T(8,128)(2,1)S(1)} collective-permute-done((bf16[4,8,5632]{2,1,0:T(8,128)(2,1)S(1)}, bf16[4,8,5632]{2,1,0:T(8,128)(2,1)S(1)}, u32[]{:S(2)}, u32[]{:S(2)}) %collective-permute-start.65) | collective-permute-done | bytes 360480 | tf_op jit(solution)/shard_map/ppermute | solution.py:22
  282.3 2.7 collective-permute-done.70
  286.4 1.6 collective-permute-start.66
  288.5 2.3 collective-permute-start.68
  291.0 5.8 %collective-permute-done.67 = bf16[8,5632]{1,0:T(8,128)(2,1)S(1)} collective-permute-done((bf16[8,5632]{1,0:T(8,128)(2,1)S(1)}, bf16[8,5632]{1,0:T(8,128)(2,1)S(1)}, u32[]{:S(2)}, u32[]{:S(2)}) %collective-permute-start.67) | collective-permute-done | bytes 90144 | tf_op jit(solution)/shard_map/ppermute | solution.py:505
  (220 shorter events, 64.4 us)
Async XLA Ops:
  14.7 15.1 %collective-permute-start = (f32[64,5632]{1,0:T(8,128)}, f32[64,5632]{1,0:T(8,128)}, u32[]{:S(2)}, u32[]{:S(2)}) collective-permute-start(f32[64,5632]{1,0:T(8,128)} %get-tuple-element.39), channel_id=1, source_target_pairs={{0,1},{1,0},{2,3},{3,2},{4,5},{5,4},{6,7},{7,6},{8,9},{9,8},{10,11... | collective-permute-start | bytes 4325384 | tf_op jit(solution)/shard_map/ppermute | solution.py:22
  25.1 2.4 collective-permute-start.1
  32.5 11.6 %collective-permute-start.2 = (bf16[4,8,5632]{2,1,0:T(8,128)(2,1)S(1)}, bf16[4,8,5632]{2,1,0:T(8,128)(2,1)S(1)}, u32[]{:S(2)}, u32[]{:S(2)}) collective-permute-start(bf16[4,8,5632]{2,1,0:T(8,128)(2,1)S(1)} %fusion.5), channel_id=1, source_target_pairs={{0,2},{1,3},{2,0},{3,1},{4,6},{5,7},{6,4},{7,5},{8,10},{9,11},{10,... | collective-permute-start | bytes 1081352 | tf_op jit(solution)/shard_map/ppermute | solution.py:22
  36.3 9.0 %collective-permute-start.6 = (bf16[2,8,2560]{2,1,0:T(8,128)(2,1)S(1)}, bf16[2,8,2560]{2,1,0:T(8,128)(2,1)S(1)}, u32[]{:S(2)}, u32[]{:S(2)}) collective-permute-start(bf16[2,8,2560]{2,1,0:T(8,128)(2,1)S(1)} %get-tuple-element.100), channel_id=1, source_target_pairs={{0,4},{1,5},{2,6},{3,7},{4,0},{5,1},{6,2},{7,3},{8,12},{9,13},{10,... | collective-permute-start | bytes 245768 | tf_op jit(solution)/shard_map/ppermute | solution.py:505
  37.9 9.4 %collective-permute-start.7 = (bf16[2,8,2560]{2,1,0:T(8,128)(2,1)S(1)}, bf16[2,8,2560]{2,1,0:T(8,128)(2,1)S(1)}, u32[]{:S(2)}, u32[]{:S(2)}) collective-permute-start(bf16[2,8,2560]{2,1,0:T(8,128)(2,1)S(1)} %get-tuple-element.99), channel_id=1, source_target_pairs={{0,8},{1,9},{2,10},{3,11},{4,12},{5,13},{6,14},{7,15},{8,0},{9,1},... | collective-permute-start | bytes 245768 | tf_op jit(solution)/shard_map/ppermute | solution.py:505
  40.5 6.9 %collective-permute-start.8 = (bf16[2,8,2560]{2,1,0:T(8,128)(2,1)S(1)}, bf16[2,8,2560]{2,1,0:T(8,128)(2,1)S(1)}, u32[]{:S(2)}, u32[]{:S(2)}) collective-permute-start(bf16[2,8,2560]{2,1,0:T(8,128)(2,1)S(1)} %get-tuple-element.98), channel_id=1, source_target_pairs={{0,12},{1,13},{2,14},{3,15},{4,8},{5,9},{6,10},{7,11},{8,4},{9,5},... | collective-permute-start | bytes 245768 | tf_op jit(solution)/shard_map/ppermute | solution.py:505
  48.3 5.0 %collective-permute-start.9 = (bf16[8,2560]{1,0:T(8,128)(2,1)S(1)}, bf16[8,2560]{1,0:T(8,128)(2,1)S(1)}, u32[]{:S(2)}, u32[]{:S(2)}) collective-permute-start(bf16[8,2560]{1,0:T(8,128)(2,1)S(1)} %fusion.80), channel_id=1, source_target_pairs={{0,2},{1,3},{2,0},{3,1},{4,6},{5,7},{6,4},{7,5},{8,10},{9,11},{10,... | collective-permute-start | bytes 122888 | tf_op jit(solution)/shard_map/ppermute | solution.py:22
  48.9 5.0 %collective-permute-start.3 = (bf16[8,5632]{1,0:T(8,128)(2,1)S(1)}, bf16[8,5632]{1,0:T(8,128)(2,1)S(1)}, u32[]{:S(2)}, u32[]{:S(2)}) collective-permute-start(bf16[8,5632]{1,0:T(8,128)(2,1)S(1)} %get-tuple-element.88), channel_id=1, source_target_pairs={{0,4},{1,5},{2,6},{3,7},{4,0},{5,1},{6,2},{7,3},{8,12},{9,13},{10,... | collective-permute-start | bytes 270344 | tf_op jit(solution)/shard_map/ppermute | solution.py:505
  50.4 9.0 %collective-permute-start.4 = (bf16[8,5632]{1,0:T(8,128)(2,1)S(1)}, bf16[8,5632]{1,0:T(8,128)(2,1)S(1)}, u32[]{:S(2)}, u32[]{:S(2)}) collective-permute-start(bf16[8,5632]{1,0:T(8,128)(2,1)S(1)} %get-tuple-element.87), channel_id=1, source_target_pairs={{0,8},{1,9},{2,10},{3,11},{4,12},{5,13},{6,14},{7,15},{8,0},{9,1},... | collective-permute-start | bytes 270344 | tf_op jit(solution)/shard_map/ppermute | solution.py:505
  52.3 7.1 %collective-permute-start.5 = (bf16[8,5632]{1,0:T(8,128)(2,1)S(1)}, bf16[8,5632]{1,0:T(8,128)(2,1)S(1)}, u32[]{:S(2)}, u32[]{:S(2)}) collective-permute-start(bf16[8,5632]{1,0:T(8,128)(2,1)S(1)} %get-tuple-element.86), channel_id=1, source_target_pairs={{0,12},{1,13},{2,14},{3,15},{4,8},{5,9},{6,10},{7,11},{8,4},{9,5},... | collective-permute-start | bytes 270344 | tf_op jit(solution)/shard_map/ppermute | solution.py:505
  59.8 6.0 %collective-permute-start.14 = (bf16[8,3072]{1,0:T(8,128)(2,1)S(1)}, bf16[8,3072]{1,0:T(8,128)(2,1)S(1)}, u32[]{:S(2)}, u32[]{:S(2)}) collective-permute-start(bf16[8,3072]{1,0:T(8,128)(2,1)S(1)} %get-tuple-element.135), channel_id=1, source_target_pairs={{0,2},{1,3},{2,0},{3,1},{4,6},{5,7},{6,4},{7,5},{8,10},{9,11},{10,... | collective-permute-start | bytes 147464 | tf_op jit(solution)/shard_map/ppermute | solution.py:22
  61.4 9.0 %collective-permute-start.10 = (bf16[8,5120]{1,0:T(8,128)(2,1)S(1)}, bf16[8,5120]{1,0:T(8,128)(2,1)S(1)}, u32[]{:S(2)}, u32[]{:S(2)}) collective-permute-start(bf16[8,5120]{1,0:T(8,128)(2,1)S(1)} %slice.84), channel_id=1, source_target_pairs={{0,8},{1,9},{2,10},{3,11},{4,12},{5,13},{6,14},{7,15},{8,0},{9,1},... | collective-permute-start | bytes 245768 | tf_op jit(solution)/shard_map/ppermute | solution.py:505
  63.3 8.9 %collective-permute-start.11 = (bf16[8,5120]{1,0:T(8,128)(2,1)S(1)}, bf16[8,5120]{1,0:T(8,128)(2,1)S(1)}, u32[]{:S(2)}, u32[]{:S(2)}) collective-permute-start(bf16[8,5120]{1,0:T(8,128)(2,1)S(1)} %slice.84), channel_id=1, source_target_pairs={{0,4},{1,5},{2,6},{3,7},{4,0},{5,1},{6,2},{7,3},{8,12},{9,13},{10,... | collective-permute-start | bytes 245768 | tf_op jit(solution)/shard_map/ppermute | solution.py:505
  63.8 8.5 %collective-permute-start.12 = (bf16[8,5120]{1,0:T(8,128)(2,1)S(1)}, bf16[8,5120]{1,0:T(8,128)(2,1)S(1)}, u32[]{:S(2)}, u32[]{:S(2)}) collective-permute-start(bf16[8,5120]{1,0:T(8,128)(2,1)S(1)} %slice.84), channel_id=1, source_target_pairs={{0,12},{1,13},{2,14},{3,15},{4,8},{5,9},{6,10},{7,11},{8,4},{9,5},... | collective-permute-start | bytes 245768 | tf_op jit(solution)/shard_map/ppermute | solution.py:505
  65.8 12.0 %collective-permute-start.15 = (bf16[2,8,3072]{2,1,0:T(8,128)(2,1)S(1)}, bf16[2,8,3072]{2,1,0:T(8,128)(2,1)S(1)}, u32[]{:S(2)}, u32[]{:S(2)}) collective-permute-start(bf16[2,8,3072]{2,1,0:T(8,128)(2,1)S(1)} %maximum_select_fusion.6), channel_id=1, source_target_pairs={{0,8},{1,9},{2,10},{3,11},{4,12},{5,13},{6,14},{7,15},{8,0},{9,1},... | collective-permute-start | bytes 294920 | tf_op jit(solution)/shard_map/ppermute | solution.py:505
  66.8 10.9 %collective-permute-start.16 = (bf16[2,8,3072]{2,1,0:T(8,128)(2,1)S(1)}, bf16[2,8,3072]{2,1,0:T(8,128)(2,1)S(1)}, u32[]{:S(2)}, u32[]{:S(2)}) collective-permute-start(bf16[2,8,3072]{2,1,0:T(8,128)(2,1)S(1)} %maximum_select_fusion.6), channel_id=1, source_target_pairs={{0,4},{1,5},{2,6},{3,7},{4,0},{5,1},{6,2},{7,3},{8,12},{9,13},{10,... | collective-permute-start | bytes 294920 | tf_op jit(solution)/shard_map/ppermute | solution.py:505
  70.4 7.4 %collective-permute-start.17 = (bf16[2,8,3072]{2,1,0:T(8,128)(2,1)S(1)}, bf16[2,8,3072]{2,1,0:T(8,128)(2,1)S(1)}, u32[]{:S(2)}, u32[]{:S(2)}) collective-permute-start(bf16[2,8,3072]{2,1,0:T(8,128)(2,1)S(1)} %maximum_select_fusion.6), channel_id=1, source_target_pairs={{0,12},{1,13},{2,14},{3,15},{4,8},{5,9},{6,10},{7,11},{8,4},{9,5},... | collective-permute-start | bytes 294920 | tf_op jit(solution)/shard_map/ppermute | solution.py:505
  72.4 7.1 %collective-permute-start.13 = (bf16[4,8,5120]{2,1,0:T(8,128)(2,1)S(1)}, bf16[4,8,5120]{2,1,0:T(8,128)(2,1)S(1)}, u32[]{:S(2)}, u32[]{:S(2)}) collective-permute-start(bf16[4,8,5120]{2,1,0:T(8,128)(2,1)S(1)} %get-tuple-element.129), channel_id=1, source_target_pairs={{0,2},{1,3},{2,0},{3,1},{4,6},{5,7},{6,4},{7,5},{8,10},{9,11},{10,... | collective-permute-start | bytes 983048 | tf_op jit(solution)/shard_map/ppermute | solution.py:22
  80.6 3.0 %collective-permute-start.18 = (bf16[4,2,8,8192]{3,2,1,0:T(8,128)(2,1)}, bf16[4,2,8,8192]{3,2,1,0:T(8,128)(2,1)}, u32[]{:S(2)}, u32[]{:S(2)}) collective-permute-start(bf16[4,2,8,8192]{3,2,1,0:T(8,128)(2,1)} %maximum_maximum_fusion), channel_id=1, source_target_pairs={{0,1},{1,0},{2,3},{3,2},{4,5},{5,4},{6,7},{7,6},{8,9},{9,8},{10,11... | collective-permute-start | bytes 3145736 | tf_op jit(solution)/shard_map/ppermute | solution.py:22
  117.1 2.9 collective-permute-start.22
  122.3 10.5 %collective-permute-start.23 = (bf16[4,8,5632]{2,1,0:T(8,128)(2,1)S(1)}, bf16[4,8,5632]{2,1,0:T(8,128)(2,1)S(1)}, u32[]{:S(2)}, u32[]{:S(2)}) collective-permute-start(bf16[4,8,5632]{2,1,0:T(8,128)(2,1)S(1)} %fusion.6), channel_id=1, source_target_pairs={{0,2},{1,3},{2,0},{3,1},{4,6},{5,7},{6,4},{7,5},{8,10},{9,11},{10,... | collective-permute-start | bytes 1081352 | tf_op jit(solution)/shard_map/ppermute | solution.py:22
  123.0 10.0 %collective-permute-start.27 = (bf16[2,8,2560]{2,1,0:T(8,128)(2,1)S(1)}, bf16[2,8,2560]{2,1,0:T(8,128)(2,1)S(1)}, u32[]{:S(2)}, u32[]{:S(2)}) collective-permute-start(bf16[2,8,2560]{2,1,0:T(8,128)(2,1)S(1)} %get-tuple-element.97), channel_id=1, source_target_pairs={{0,4},{1,5},{2,6},{3,7},{4,0},{5,1},{6,2},{7,3},{8,12},{9,13},{10,... | collective-permute-start | bytes 245768 | tf_op jit(solution)/shard_map/ppermute | solution.py:505
  126.3 9.1 %collective-permute-start.28 = (bf16[2,8,2560]{2,1,0:T(8,128)(2,1)S(1)}, bf16[2,8,2560]{2,1,0:T(8,128)(2,1)S(1)}, u32[]{:S(2)}, u32[]{:S(2)}) collective-permute-start(bf16[2,8,2560]{2,1,0:T(8,128)(2,1)S(1)} %get-tuple-element.96), channel_id=1, source_target_pairs={{0,8},{1,9},{2,10},{3,11},{4,12},{5,13},{6,14},{7,15},{8,0},{9,1},... | collective-permute-start | bytes 245768 | tf_op jit(solution)/shard_map/ppermute | solution.py:505
  126.9 8.5 %collective-permute-start.29 = (bf16[2,8,2560]{2,1,0:T(8,128)(2,1)S(1)}, bf16[2,8,2560]{2,1,0:T(8,128)(2,1)S(1)}, u32[]{:S(2)}, u32[]{:S(2)}) collective-permute-start(bf16[2,8,2560]{2,1,0:T(8,128)(2,1)S(1)} %get-tuple-element.95), channel_id=1, source_target_pairs={{0,12},{1,13},{2,14},{3,15},{4,8},{5,9},{6,10},{7,11},{8,4},{9,5},... | collective-permute-start | bytes 245768 | tf_op jit(solution)/shard_map/ppermute | solution.py:505
  135.5 5.9 %collective-permute-start.30 = (bf16[8,2560]{1,0:T(8,128)(2,1)S(1)}, bf16[8,2560]{1,0:T(8,128)(2,1)S(1)}, u32[]{:S(2)}, u32[]{:S(2)}) collective-permute-start(bf16[8,2560]{1,0:T(8,128)(2,1)S(1)} %fusion.81), channel_id=1, source_target_pairs={{0,2},{1,3},{2,0},{3,1},{4,6},{5,7},{6,4},{7,5},{8,10},{9,11},{10,... | collective-permute-start | bytes 122888 | tf_op jit(solution)/shard_map/ppermute | solution.py:22
  137.0 4.7 %collective-permute-start.24 = (bf16[8,5632]{1,0:T(8,128)(2,1)S(1)}, bf16[8,5632]{1,0:T(8,128)(2,1)S(1)}, u32[]{:S(2)}, u32[]{:S(2)}) collective-permute-start(bf16[8,5632]{1,0:T(8,128)(2,1)S(1)} %get-tuple-element.85), channel_id=1, source_target_pairs={{0,4},{1,5},{2,6},{3,7},{4,0},{5,1},{6,2},{7,3},{8,12},{9,13},{10,... | collective-permute-start | bytes 270344 | tf_op jit(solution)/shard_map/ppermute | solution.py:505
  138.6 8.9 %collective-permute-start.25 = (bf16[8,5632]{1,0:T(8,128)(2,1)S(1)}, bf16[8,5632]{1,0:T(8,128)(2,1)S(1)}, u32[]{:S(2)}, u32[]{:S(2)}) collective-permute-start(bf16[8,5632]{1,0:T(8,128)(2,1)S(1)} %get-tuple-element.84), channel_id=1, source_target_pairs={{0,8},{1,9},{2,10},{3,11},{4,12},{5,13},{6,14},{7,15},{8,0},{9,1},... | collective-permute-start | bytes 270344 | tf_op jit(solution)/shard_map/ppermute | solution.py:505
  139.5 8.1 %collective-permute-start.26 = (bf16[8,5632]{1,0:T(8,128)(2,1)S(1)}, bf16[8,5632]{1,0:T(8,128)(2,1)S(1)}, u32[]{:S(2)}, u32[]{:S(2)}) collective-permute-start(bf16[8,5632]{1,0:T(8,128)(2,1)S(1)} %get-tuple-element.83), channel_id=1, source_target_pairs={{0,12},{1,13},{2,14},{3,15},{4,8},{5,9},{6,10},{7,11},{8,4},{9,5},... | collective-permute-start | bytes 270344 | tf_op jit(solution)/shard_map/ppermute | solution.py:505
  147.9 5.1 %collective-permute-start.35 = (bf16[8,3072]{1,0:T(8,128)(2,1)S(1)}, bf16[8,3072]{1,0:T(8,128)(2,1)S(1)}, u32[]{:S(2)}, u32[]{:S(2)}) collective-permute-start(bf16[8,3072]{1,0:T(8,128)(2,1)S(1)} %get-tuple-element.133), channel_id=1, source_target_pairs={{0,2},{1,3},{2,0},{3,1},{4,6},{5,7},{6,4},{7,5},{8,10},{9,11},{10,... | collective-permute-start | bytes 147464 | tf_op jit(solution)/shard_map/ppermute | solution.py:22
  148.6 8.6 %collective-permute-start.31 = (bf16[8,5120]{1,0:T(8,128)(2,1)S(1)}, bf16[8,5120]{1,0:T(8,128)(2,1)S(1)}, u32[]{:S(2)}, u32[]{:S(2)}) collective-permute-start(bf16[8,5120]{1,0:T(8,128)(2,1)S(1)} %slice.90), channel_id=1, source_target_pairs={{0,8},{1,9},{2,10},{3,11},{4,12},{5,13},{6,14},{7,15},{8,0},{9,1},... | collective-permute-start | bytes 245768 | tf_op jit(solution)/shard_map/ppermute | solution.py:505
  150.8 8.8 %collective-permute-start.32 = (bf16[8,5120]{1,0:T(8,128)(2,1)S(1)}, bf16[8,5120]{1,0:T(8,128)(2,1)S(1)}, u32[]{:S(2)}, u32[]{:S(2)}) collective-permute-start(bf16[8,5120]{1,0:T(8,128)(2,1)S(1)} %slice.90), channel_id=1, source_target_pairs={{0,4},{1,5},{2,6},{3,7},{4,0},{5,1},{6,2},{7,3},{8,12},{9,13},{10,... | collective-permute-start | bytes 245768 | tf_op jit(solution)/shard_map/ppermute | solution.py:505
  151.1 8.5 %collective-permute-start.33 = (bf16[8,5120]{1,0:T(8,128)(2,1)S(1)}, bf16[8,5120]{1,0:T(8,128)(2,1)S(1)}, u32[]{:S(2)}, u32[]{:S(2)}) collective-permute-start(bf16[8,5120]{1,0:T(8,128)(2,1)S(1)} %slice.90), channel_id=1, source_target_pairs={{0,12},{1,13},{2,14},{3,15},{4,8},{5,9},{6,10},{7,11},{8,4},{9,5},... | collective-permute-start | bytes 245768 | tf_op jit(solution)/shard_map/ppermute | solution.py:505
  153.0 12.3 %collective-permute-start.36 = (bf16[2,8,3072]{2,1,0:T(8,128)(2,1)S(1)}, bf16[2,8,3072]{2,1,0:T(8,128)(2,1)S(1)}, u32[]{:S(2)}, u32[]{:S(2)}) collective-permute-start(bf16[2,8,3072]{2,1,0:T(8,128)(2,1)S(1)} %maximum_select_fusion.7), channel_id=1, source_target_pairs={{0,8},{1,9},{2,10},{3,11},{4,12},{5,13},{6,14},{7,15},{8,0},{9,1},... | collective-permute-start | bytes 294920 | tf_op jit(solution)/shard_map/ppermute | solution.py:505
  154.3 11.0 %collective-permute-start.37 = (bf16[2,8,3072]{2,1,0:T(8,128)(2,1)S(1)}, bf16[2,8,3072]{2,1,0:T(8,128)(2,1)S(1)}, u32[]{:S(2)}, u32[]{:S(2)}) collective-permute-start(bf16[2,8,3072]{2,1,0:T(8,128)(2,1)S(1)} %maximum_select_fusion.7), channel_id=1, source_target_pairs={{0,4},{1,5},{2,6},{3,7},{4,0},{5,1},{6,2},{7,3},{8,12},{9,13},{10,... | collective-permute-start | bytes 294920 | tf_op jit(solution)/shard_map/ppermute | solution.py:505
  157.2 8.1 %collective-permute-start.38 = (bf16[2,8,3072]{2,1,0:T(8,128)(2,1)S(1)}, bf16[2,8,3072]{2,1,0:T(8,128)(2,1)S(1)}, u32[]{:S(2)}, u32[]{:S(2)}) collective-permute-start(bf16[2,8,3072]{2,1,0:T(8,128)(2,1)S(1)} %maximum_select_fusion.7), channel_id=1, source_target_pairs={{0,12},{1,13},{2,14},{3,15},{4,8},{5,9},{6,10},{7,11},{8,4},{9,5},... | collective-permute-start | bytes 294920 | tf_op jit(solution)/shard_map/ppermute | solution.py:505
  159.7 7.1 %collective-permute-start.34 = (bf16[4,8,5120]{2,1,0:T(8,128)(2,1)S(1)}, bf16[4,8,5120]{2,1,0:T(8,128)(2,1)S(1)}, u32[]{:S(2)}, u32[]{:S(2)}) collective-permute-start(bf16[4,8,5120]{2,1,0:T(8,128)(2,1)S(1)} %get-tuple-element.127), channel_id=1, source_target_pairs={{0,2},{1,3},{2,0},{3,1},{4,6},{5,7},{6,4},{7,5},{8,10},{9,11},{10,... | collective-permute-start | bytes 983048 | tf_op jit(solution)/shard_map/ppermute | solution.py:22
  167.2 2.7 collective-permute-start.39
  193.9 2.7 collective-permute-start.43
  197.1 10.5 %collective-permute-start.44 = (bf16[4,8,5632]{2,1,0:T(8,128)(2,1)S(1)}, bf16[4,8,5632]{2,1,0:T(8,128)(2,1)S(1)}, u32[]{:S(2)}, u32[]{:S(2)}) collective-permute-start(bf16[4,8,5632]{2,1,0:T(8,128)(2,1)S(1)} %fusion.7), channel_id=1, source_target_pairs={{0,2},{1,3},{2,0},{3,1},{4,6},{5,7},{6,4},{7,5},{8,10},{9,11},{10,... | collective-permute-start | bytes 1081352 | tf_op jit(solution)/shard_map/ppermute | solution.py:22
  198.6 9.1 %collective-permute-start.48 = (bf16[2,8,2560]{2,1,0:T(8,128)(2,1)S(1)}, bf16[2,8,2560]{2,1,0:T(8,128)(2,1)S(1)}, u32[]{:S(2)}, u32[]{:S(2)}) collective-permute-start(bf16[2,8,2560]{2,1,0:T(8,128)(2,1)S(1)} %get-tuple-element.94), channel_id=1, source_target_pairs={{0,4},{1,5},{2,6},{3,7},{4,0},{5,1},{6,2},{7,3},{8,12},{9,13},{10,... | collective-permute-start | bytes 245768 | tf_op jit(solution)/shard_map/ppermute | solution.py:505
  202.2 9.0 %collective-permute-start.49 = (bf16[2,8,2560]{2,1,0:T(8,128)(2,1)S(1)}, bf16[2,8,2560]{2,1,0:T(8,128)(2,1)S(1)}, u32[]{:S(2)}, u32[]{:S(2)}) collective-permute-start(bf16[2,8,2560]{2,1,0:T(8,128)(2,1)S(1)} %get-tuple-element.93), channel_id=1, source_target_pairs={{0,8},{1,9},{2,10},{3,11},{4,12},{5,13},{6,14},{7,15},{8,0},{9,1},... | collective-permute-start | bytes 245768 | tf_op jit(solution)/shard_map/ppermute | solution.py:505
  202.2 9.0 %collective-permute-start.50 = (bf16[2,8,2560]{2,1,0:T(8,128)(2,1)S(1)}, bf16[2,8,2560]{2,1,0:T(8,128)(2,1)S(1)}, u32[]{:S(2)}, u32[]{:S(2)}) collective-permute-start(bf16[2,8,2560]{2,1,0:T(8,128)(2,1)S(1)} %get-tuple-element.92), channel_id=1, source_target_pairs={{0,12},{1,13},{2,14},{3,15},{4,8},{5,9},{6,10},{7,11},{8,4},{9,5},... | collective-permute-start | bytes 245768 | tf_op jit(solution)/shard_map/ppermute | solution.py:505
  211.3 4.8 %collective-permute-start.51 = (bf16[8,2560]{1,0:T(8,128)(2,1)S(1)}, bf16[8,2560]{1,0:T(8,128)(2,1)S(1)}, u32[]{:S(2)}, u32[]{:S(2)}) collective-permute-start(bf16[8,2560]{1,0:T(8,128)(2,1)S(1)} %fusion.82), channel_id=1, source_target_pairs={{0,2},{1,3},{2,0},{3,1},{4,6},{5,7},{6,4},{7,5},{8,10},{9,11},{10,... | collective-permute-start | bytes 122888 | tf_op jit(solution)/shard_map/ppermute | solution.py:22
  211.7 5.0 %collective-permute-start.45 = (bf16[8,5632]{1,0:T(8,128)(2,1)S(1)}, bf16[8,5632]{1,0:T(8,128)(2,1)S(1)}, u32[]{:S(2)}, u32[]{:S(2)}) collective-permute-start(bf16[8,5632]{1,0:T(8,128)(2,1)S(1)} %get-tuple-element.82), channel_id=1, source_target_pairs={{0,4},{1,5},{2,6},{3,7},{4,0},{5,1},{6,2},{7,3},{8,12},{9,13},{10,... | collective-permute-start | bytes 270344 | tf_op jit(solution)/shard_map/ppermute | solution.py:505
  213.3 9.0 %collective-permute-start.46 = (bf16[8,5632]{1,0:T(8,128)(2,1)S(1)}, bf16[8,5632]{1,0:T(8,128)(2,1)S(1)}, u32[]{:S(2)}, u32[]{:S(2)}) collective-permute-start(bf16[8,5632]{1,0:T(8,128)(2,1)S(1)} %get-tuple-element.81), channel_id=1, source_target_pairs={{0,8},{1,9},{2,10},{3,11},{4,12},{5,13},{6,14},{7,15},{8,0},{9,1},... | collective-permute-start | bytes 270344 | tf_op jit(solution)/shard_map/ppermute | solution.py:505
  214.3 8.0 %collective-permute-start.47 = (bf16[8,5632]{1,0:T(8,128)(2,1)S(1)}, bf16[8,5632]{1,0:T(8,128)(2,1)S(1)}, u32[]{:S(2)}, u32[]{:S(2)}) collective-permute-start(bf16[8,5632]{1,0:T(8,128)(2,1)S(1)} %get-tuple-element.80), channel_id=1, source_target_pairs={{0,12},{1,13},{2,14},{3,15},{4,8},{5,9},{6,10},{7,11},{8,4},{9,5},... | collective-permute-start | bytes 270344 | tf_op jit(solution)/shard_map/ppermute | solution.py:505
  222.7 5.8 %collective-permute-start.56 = (bf16[8,3072]{1,0:T(8,128)(2,1)S(1)}, bf16[8,3072]{1,0:T(8,128)(2,1)S(1)}, u32[]{:S(2)}, u32[]{:S(2)}) collective-permute-start(bf16[8,3072]{1,0:T(8,128)(2,1)S(1)} %get-tuple-element.131), channel_id=1, source_target_pairs={{0,2},{1,3},{2,0},{3,1},{4,6},{5,7},{6,4},{7,5},{8,10},{9,11},{10,... | collective-permute-start | bytes 147464 | tf_op jit(solution)/shard_map/ppermute | solution.py:22
  224.1 9.1 %collective-permute-start.52 = (bf16[8,5120]{1,0:T(8,128)(2,1)S(1)}, bf16[8,5120]{1,0:T(8,128)(2,1)S(1)}, u32[]{:S(2)}, u32[]{:S(2)}) collective-permute-start(bf16[8,5120]{1,0:T(8,128)(2,1)S(1)} %slice.97), channel_id=1, source_target_pairs={{0,8},{1,9},{2,10},{3,11},{4,12},{5,13},{6,14},{7,15},{8,0},{9,1},... | collective-permute-start | bytes 245768 | tf_op jit(solution)/shard_map/ppermute | solution.py:505
  225.6 8.0 %collective-permute-start.53 = (bf16[8,5120]{1,0:T(8,128)(2,1)S(1)}, bf16[8,5120]{1,0:T(8,128)(2,1)S(1)}, u32[]{:S(2)}, u32[]{:S(2)}) collective-permute-start(bf16[8,5120]{1,0:T(8,128)(2,1)S(1)} %slice.97), channel_id=1, source_target_pairs={{0,4},{1,5},{2,6},{3,7},{4,0},{5,1},{6,2},{7,3},{8,12},{9,13},{10,... | collective-permute-start | bytes 245768 | tf_op jit(solution)/shard_map/ppermute | solution.py:505
  226.1 8.8 %collective-permute-start.54 = (bf16[8,5120]{1,0:T(8,128)(2,1)S(1)}, bf16[8,5120]{1,0:T(8,128)(2,1)S(1)}, u32[]{:S(2)}, u32[]{:S(2)}) collective-permute-start(bf16[8,5120]{1,0:T(8,128)(2,1)S(1)} %slice.97), channel_id=1, source_target_pairs={{0,12},{1,13},{2,14},{3,15},{4,8},{5,9},{6,10},{7,11},{8,4},{9,5},... | collective-permute-start | bytes 245768 | tf_op jit(solution)/shard_map/ppermute | solution.py:505
  228.5 12.5 %collective-permute-start.57 = (bf16[2,8,3072]{2,1,0:T(8,128)(2,1)S(1)}, bf16[2,8,3072]{2,1,0:T(8,128)(2,1)S(1)}, u32[]{:S(2)}, u32[]{:S(2)}) collective-permute-start(bf16[2,8,3072]{2,1,0:T(8,128)(2,1)S(1)} %maximum_select_fusion.8), channel_id=1, source_target_pairs={{0,8},{1,9},{2,10},{3,11},{4,12},{5,13},{6,14},{7,15},{8,0},{9,1},... | collective-permute-start | bytes 294920 | tf_op jit(solution)/shard_map/ppermute | solution.py:505
  229.2 11.8 %collective-permute-start.58 = (bf16[2,8,3072]{2,1,0:T(8,128)(2,1)S(1)}, bf16[2,8,3072]{2,1,0:T(8,128)(2,1)S(1)}, u32[]{:S(2)}, u32[]{:S(2)}) collective-permute-start(bf16[2,8,3072]{2,1,0:T(8,128)(2,1)S(1)} %maximum_select_fusion.8), channel_id=1, source_target_pairs={{0,4},{1,5},{2,6},{3,7},{4,0},{5,1},{6,2},{7,3},{8,12},{9,13},{10,... | collective-permute-start | bytes 294920 | tf_op jit(solution)/shard_map/ppermute | solution.py:505
  233.2 7.8 %collective-permute-start.59 = (bf16[2,8,3072]{2,1,0:T(8,128)(2,1)S(1)}, bf16[2,8,3072]{2,1,0:T(8,128)(2,1)S(1)}, u32[]{:S(2)}, u32[]{:S(2)}) collective-permute-start(bf16[2,8,3072]{2,1,0:T(8,128)(2,1)S(1)} %maximum_select_fusion.8), channel_id=1, source_target_pairs={{0,12},{1,13},{2,14},{3,15},{4,8},{5,9},{6,10},{7,11},{8,4},{9,5},... | collective-permute-start | bytes 294920 | tf_op jit(solution)/shard_map/ppermute | solution.py:505
  235.0 7.1 %collective-permute-start.55 = (bf16[4,8,5120]{2,1,0:T(8,128)(2,1)S(1)}, bf16[4,8,5120]{2,1,0:T(8,128)(2,1)S(1)}, u32[]{:S(2)}, u32[]{:S(2)}) collective-permute-start(bf16[4,8,5120]{2,1,0:T(8,128)(2,1)S(1)} %get-tuple-element.125), channel_id=1, source_target_pairs={{0,2},{1,3},{2,0},{3,1},{4,6},{5,7},{6,4},{7,5},{8,10},{9,11},{10,... | collective-permute-start | bytes 983048 | tf_op jit(solution)/shard_map/ppermute | solution.py:22
  242.5 2.7 collective-permute-start.60
  268.5 2.7 collective-permute-start.64
  271.7 10.5 %collective-permute-start.65 = (bf16[4,8,5632]{2,1,0:T(8,128)(2,1)S(1)}, bf16[4,8,5632]{2,1,0:T(8,128)(2,1)S(1)}, u32[]{:S(2)}, u32[]{:S(2)}) collective-permute-start(bf16[4,8,5632]{2,1,0:T(8,128)(2,1)S(1)} %fusion.8), channel_id=1, source_target_pairs={{0,2},{1,3},{2,0},{3,1},{4,6},{5,7},{6,4},{7,5},{8,10},{9,11},{10,... | collective-permute-start | bytes 1081352 | tf_op jit(solution)/shard_map/ppermute | solution.py:22
  272.7 9.6 %collective-permute-start.69 = (bf16[2,8,2560]{2,1,0:T(8,128)(2,1)S(1)}, bf16[2,8,2560]{2,1,0:T(8,128)(2,1)S(1)}, u32[]{:S(2)}, u32[]{:S(2)}) collective-permute-start(bf16[2,8,2560]{2,1,0:T(8,128)(2,1)S(1)} %get-tuple-element.91), channel_id=1, source_target_pairs={{0,4},{1,5},{2,6},{3,7},{4,0},{5,1},{6,2},{7,3},{8,12},{9,13},{10,... | collective-permute-start | bytes 245768 | tf_op jit(solution)/shard_map/ppermute | solution.py:505
  275.8 9.2 %collective-permute-start.70 = (bf16[2,8,2560]{2,1,0:T(8,128)(2,1)S(1)}, bf16[2,8,2560]{2,1,0:T(8,128)(2,1)S(1)}, u32[]{:S(2)}, u32[]{:S(2)}) collective-permute-start(bf16[2,8,2560]{2,1,0:T(8,128)(2,1)S(1)} %get-tuple-element.90), channel_id=1, source_target_pairs={{0,8},{1,9},{2,10},{3,11},{4,12},{5,13},{6,14},{7,15},{8,0},{9,1},... | collective-permute-start | bytes 245768 | tf_op jit(solution)/shard_map/ppermute | solution.py:505
  276.7 8.3 %collective-permute-start.71 = (bf16[2,8,2560]{2,1,0:T(8,128)(2,1)S(1)}, bf16[2,8,2560]{2,1,0:T(8,128)(2,1)S(1)}, u32[]{:S(2)}, u32[]{:S(2)}) collective-permute-start(bf16[2,8,2560]{2,1,0:T(8,128)(2,1)S(1)} %get-tuple-element.89), channel_id=1, source_target_pairs={{0,12},{1,13},{2,14},{3,15},{4,8},{5,9},{6,10},{7,11},{8,4},{9,5},... | collective-permute-start | bytes 245768 | tf_op jit(solution)/shard_map/ppermute | solution.py:505
  285.1 5.7 %collective-permute-start.72 = (bf16[8,2560]{1,0:T(8,128)(2,1)S(1)}, bf16[8,2560]{1,0:T(8,128)(2,1)S(1)}, u32[]{:S(2)}, u32[]{:S(2)}) collective-permute-start(bf16[8,2560]{1,0:T(8,128)(2,1)S(1)} %fusion.83), channel_id=1, source_target_pairs={{0,2},{1,3},{2,0},{3,1},{4,6},{5,7},{6,4},{7,5},{8,10},{9,11},{10,... | collective-permute-start | bytes 122888 | tf_op jit(solution)/shard_map/ppermute | solution.py:22
  286.4 4.6 %collective-permute-start.66 = (bf16[8,5632]{1,0:T(8,128)(2,1)S(1)}, bf16[8,5632]{1,0:T(8,128)(2,1)S(1)}, u32[]{:S(2)}, u32[]{:S(2)}) collective-permute-start(bf16[8,5632]{1,0:T(8,128)(2,1)S(1)} %get-tuple-element.79), channel_id=1, source_target_pairs={{0,4},{1,5},{2,6},{3,7},{4,0},{5,1},{6,2},{7,3},{8,12},{9,13},{10,... | collective-permute-start | bytes 270344 | tf_op jit(solution)/shard_map/ppermute | solution.py:505
  288.0 8.7 %collective-permute-start.67 = (bf16[8,5632]{1,0:T(8,128)(2,1)S(1)}, bf16[8,5632]{1,0:T(8,128)(2,1)S(1)}, u32[]{:S(2)}, u32[]{:S(2)}) collective-permute-start(bf16[8,5632]{1,0:T(8,128)(2,1)S(1)} %get-tuple-element.78), channel_id=1, source_target_pairs={{0,8},{1,9},{2,10},{3,11},{4,12},{5,13},{6,14},{7,15},{8,0},{9,1},... | collective-permute-start | bytes 270344 | tf_op jit(solution)/shard_map/ppermute | solution.py:505
  288.5 8.3 %collective-permute-start.68 = (bf16[8,5632]{1,0:T(8,128)(2,1)S(1)}, bf16[8,5632]{1,0:T(8,128)(2,1)S(1)}, u32[]{:S(2)}, u32[]{:S(2)}) collective-permute-start(bf16[8,5632]{1,0:T(8,128)(2,1)S(1)} %get-tuple-element.77), channel_id=1, source_target_pairs={{0,12},{1,13},{2,14},{3,15},{4,8},{5,9},{6,10},{7,11},{8,4},{9,5},... | collective-permute-start | bytes 270344 | tf_op jit(solution)/shard_map/ppermute | solution.py:505
  (23 other events, 235.1 us)

commit v2 on v0

--- a/solution.py
+++ b/solution.py
@@ -556,7 +556,7 @@
     side = (lax.axis_index("tensor") % 2).astype(jnp.int32)
     row_count = tapped.shape[0]
     columns = join_weight.shape[1]
-    sum_cut, cut = columns * 11 // 16, columns * 5 // 8
+    sum_cut, cut = columns * 3 // 4, columns * 5 // 8
     spans = ((0, sum_cut), (sum_cut, columns))
     seq_count, piece_len = kv_cache.shape[:2]
     node_count = row_count // seq_count

time: 296 us -> 297 us (level)
  starting transfers between devices: 84.1 us -> 92 us
  waiting for transfers between devices: 100 us -> 93.9 us
    ppermute x42, waiting for transfers between devices: 56.6 us -> 46.1 us  [across_depth(): lax.ppermute(x, 'tensor', [(i, i ^ k << DEEP) for i in range(lax.axis_siz...]
    ppermute x42, starting transfers between devices: 64.4 us -> 71 us  [across_depth(): lax.ppermute(x, 'tensor', [(i, i ^ k << DEEP) for i in range(lax.axis_siz...]
    ppermute x31, waiting for transfers between devices: 43.5 us -> 47.8 us  [partner(): lax.ppermute(x, axis, [(i, i ^ 1 << distance) for i in range(lax.axis_siz...]
    unnamed x28 -> x30, local copies, waits for them, and re-layouts: 5.64 us -> 5.96 us
  transfers between devices with their start and end apart: 73 -> 73, of which waited for: 40 -> 37; matrix products, arithmetic and copies ran while one was open for 3% -> 2% of each run, Pallas kernels for 3% -> 2%
where the time goes in v2:
time: 297 us; the launch traced here: 294 us
  waiting for transfers between devices  93.9 us (32%)
  starting transfers between devices  92 us (31%)
  Pallas kernels  67.9 us (23%)
  matrix products  17.3 us (6%)
  other arithmetic  14.6 us (5%)
  local copies, waits for them, and re-layouts  7.62 us (3%)
    ppermute x42, starting transfers between devices, across_depth(): lax.ppermute(x, 'tensor', [(i, i ^ k << DEEP) for i in range(lax.axis_siz...  71 us
    ppermute x31, waiting for transfers between devices, partner(): lax.ppermute(x, axis, [(i, i ^ 1 << distance) for i in range(lax.axis_siz...  47.8 us
    pallas_call x3, Pallas kernels, attend(): pl.pallas_call(functools.partial(attend_kernel, depth), out_shape=(jax.Sh...  47.6 us
    ppermute x42, waiting for transfers between devices, across_depth(): lax.ppermute(x, 'tensor', [(i, i ^ k << DEEP) for i in range(lax.axis_siz...  46.1 us
    ppermute x31, starting transfers between devices, partner(): lax.ppermute(x, axis, [(i, i ^ 1 << distance) for i in range(lax.axis_siz...  21.1 us
    pallas_call x2, Pallas kernels, join(): pl.pallas_call(functools.partial(join_kernel, start), out_shape=(out, out...  20.3 us
    dot_general x3, matrix products, local_pairs(): jnp.dot(attended.astype(jnp.bfloat16), out_weight, preferred_element_type...  7.61 us
    dot_general x3, matrix products, local_pairs(): query = jnp.dot(normed, query_weight, preferred_element_type=jnp.float32)  7.16 us
  transfers between devices with their start and end apart: 73, of which 37 were waited for; matrix products, arithmetic and copies ran while one was open for 2% of the time, Pallas kernels for 2%

profile of v2, /device:TPU:0, one launch (start us, length us, event | category | flops | bytes accessed | tf_op | source)
XLA Modules:
  0.0 294.2 jit_solution(13854496583101483871)
XLA Ops:
  1.3 14.1 %join.2 = (f32[64,6144]{1,0:T(8,128)S(1)}, f32[64,6144]{1,0:T(8,128)}) custom-call(s32[1]{0:T(128)} %bitcast.side_ref, bf16[128,3072]{1,0:T(8,128)(2,1)S(1)} %copy-done.1, bf16[3072,8192]{1,0:T(8,128)(2,1)} %weight_ref.3), custom_call_target="tpu_custom_call" | custom-call | flops 4831838208 | bytes 37748736 | tf_op jit(solution)/shard_map/join/pallas_call | solution.py:452
  17.0 6.2 %join.3 = (f32[64,2048]{1,0:T(8,128)S(1)}, f32[64,2048]{1,0:T(8,128)S(1)}) custom-call(s32[1]{0:T(128)} %bitcast.side_ref, bf16[128,3072]{1,0:T(8,128)(2,1)S(1)} %copy-done.1, bf16[3072,8192]{1,0:T(8,128)(2,1)} %weight_ref.3), custom_call_target="tpu_custom_call" | custom-call | flops 1610612736 | bytes 12582912 | tf_op jit(solution)/shard_map/join/pallas_call | solution.py:452
  23.3 2.0 collective-permute-done.1
  26.4 1.7 add.285
  29.2 2.7 collective-permute-start.2
  32.0 1.7 collective-permute-start.6
  33.6 2.6 collective-permute-start.7
  36.4 5.2 %collective-permute-done.2 = bf16[4,8,6144]{2,1,0:T(8,128)(2,1)S(1)} collective-permute-done((bf16[4,8,6144]{2,1,0:T(8,128)(2,1)S(1)}, bf16[4,8,6144]{2,1,0:T(8,128)(2,1)S(1)}, u32[]{:S(2)}, u32[]{:S(2)}) %collective-permute-start.2) | collective-permute-done | bytes 393248 | tf_op jit(solution)/shard_map/ppermute | solution.py:22
  42.9 1.8 collective-permute-start.9
  44.7 1.6 collective-permute-start.3
  46.3 2.6 collective-permute-start.4
  50.3 5.9 %collective-permute-done.4 = bf16[8,6144]{1,0:T(8,128)(2,1)S(1)} collective-permute-done((bf16[8,6144]{1,0:T(8,128)(2,1)S(1)}, bf16[8,6144]{1,0:T(8,128)(2,1)S(1)}, u32[]{:S(2)}, u32[]{:S(2)}) %collective-permute-start.4) | collective-permute-done | bytes 98336 | tf_op jit(solution)/shard_map/ppermute | solution.py:505
  57.2 2.6 collective-permute-start.10
  61.6 1.8 collective-permute-start.15
  66.2 2.3 collective-permute-start.17
  70.2 3.8 %collective-permute-done.15 = bf16[2,8,3072]{2,1,0:T(8,128)(2,1)S(1)} collective-permute-done((bf16[2,8,3072]{2,1,0:T(8,128)(2,1)S(1)}, bf16[2,8,3072]{2,1,0:T(8,128)(2,1)S(1)}, u32[]{:S(2)}, u32[]{:S(2)}) %collective-permute-start.15) | collective-permute-done | bytes 98336 | tf_op jit(solution)/shard_map/ppermute | solution.py:505
  77.1 2.8 collective-permute-done.18
  79.9 1.8 maximum_select_fusion
  81.7 4.6 %convolution_convert_fusion.2.mine_ref = bf16[128,512]{1,0:T(8,128)(2,1)S(1)} fusion(bf16[128,8192]{1,0:T(8,128)(2,1)S(1)} %bitcast.265, bf16[8192,512]{1,0:T(8,128)(2,1)} %param.12), kind=kOutput, calls=%fused_computation.11 | convolution fusion | flops 1073807360 | bytes 10616832 | tf_op jit(solution)/shard_map/dot_general | solution.py:588
  88.6 15.6 %attend.3 = (f32[128,512]{1,0:T(8,128)S(1)}, f32[128,512]{1,0:T(8,128)S(1)}, f32[128,1024]{1,0:T(8,128)S(1)}) custom-call(s32[3]{0:T(128)S(1)} %pad_add_fusion.info_ref, bf16[128,512]{1,0:T(8,128)(2,1)S(1)} %convolution_convert_fusion.2.mine_ref, bf16[128,512]{1,0:T(8,128)(2,1)S(1)} %collective-permute-done.19.other_ref, ...), custom_call_target="tpu_custom_call" | custom-call | flops 8589934592 | bytes 16777216 | tf_op jit(solution)/shard_map/attend/pallas_call | solution.py:367
  104.3 2.0 collective-permute-done.21
  106.3 4.9 %fusion.42 = f32[128,8192]{1,0:T(8,128)S(1)} fusion(bf16[512,8192]{1,0:T(8,128)(2,1)} %param.14, f32[128,1024]{1,0:T(8,128)} %collective-permute-done.21, f32[128,512]{1,0:T(8,128)S(1)} %get-tuple-element.49, f32[128,512]{1,0:T(8,128)S(1)} %get-tuple-element.47), kind=kOutput, calls=%fused_computation.111 | convolution fusion | flops 1074462720 | bytes 13631488 | tf_op jit(solution)/shard_map/dot_general | solution.py:602
  111.2 2.0 copy-done.4
  113.6 2.6 collective-permute-done.22
  116.2 2.1 bitcast_add_fusion.2
  118.5 1.6 collective-permute-start.23
  120.1 3.1 %collective-permute-start.27 = (bf16[2,8,2048]{2,1,0:T(8,128)(2,1)S(1)}, bf16[2,8,2048]{2,1,0:T(8,128)(2,1)S(1)}, u32[]{:S(2)}, u32[]{:S(2)}) collective-permute-start(bf16[2,8,2048]{2,1,0:T(8,128)(2,1)S(1)} %get-tuple-element.97), channel_id=1, source_target_pairs={{0,4},{1,5},{2,6},{3,7},{4,0},{5,1},{6,2},{7,3},{8,12},{9,13},{10,... | collective-permute-start | bytes 196616 | tf_op jit(solution)/shard_map/ppermute | solution.py:505
  124.0 1.6 collective-permute-start.29
  125.6 4.1 %collective-permute-done.23 = bf16[4,8,6144]{2,1,0:T(8,128)(2,1)S(1)} collective-permute-done((bf16[4,8,6144]{2,1,0:T(8,128)(2,1)S(1)}, bf16[4,8,6144]{2,1,0:T(8,128)(2,1)S(1)}, u32[]{:S(2)}, u32[]{:S(2)}) %collective-permute-start.23) | collective-permute-done | bytes 393248 | tf_op jit(solution)/shard_map/ppermute | solution.py:22
  131.8 2.7 collective-permute-start.24
  135.3 1.6 collective-permute-start.26
  137.9 6.2 %collective-permute-done.25 = bf16[8,6144]{1,0:T(8,128)(2,1)S(1)} collective-permute-done((bf16[8,6144]{1,0:T(8,128)(2,1)S(1)}, bf16[8,6144]{1,0:T(8,128)(2,1)S(1)}, u32[]{:S(2)}, u32[]{:S(2)}) %collective-permute-start.25) | collective-permute-done | bytes 98336 | tf_op jit(solution)/shard_map/ppermute | solution.py:505
  145.1 2.4 collective-permute-start.31
  147.6 1.9 collective-permute-start.33
  149.5 1.6 collective-permute-start.36
  152.7 3.7 %collective-permute-start.38 = (bf16[2,8,3072]{2,1,0:T(8,128)(2,1)S(1)}, bf16[2,8,3072]{2,1,0:T(8,128)(2,1)S(1)}, u32[]{:S(2)}, u32[]{:S(2)}) collective-permute-start(bf16[2,8,3072]{2,1,0:T(8,128)(2,1)S(1)} %maximum_select_fusion.7), channel_id=1, source_target_pairs={{0,12},{1,13},{2,14},{3,15},{4,8},{5,9},{6,10},{7,11},{8,4},{9,5},... | collective-permute-start | bytes 294920 | tf_op jit(solution)/shard_map/ppermute | solution.py:505
  158.1 3.5 %collective-permute-done.36 = bf16[2,8,3072]{2,1,0:T(8,128)(2,1)S(1)} collective-permute-done((bf16[2,8,3072]{2,1,0:T(8,128)(2,1)S(1)}, bf16[2,8,3072]{2,1,0:T(8,128)(2,1)S(1)}, u32[]{:S(2)}, u32[]{:S(2)}) %collective-permute-start.36) | collective-permute-done | bytes 98336 | tf_op jit(solution)/shard_map/ppermute | solution.py:505
  161.7 2.0 collective-permute-done.34
  164.5 2.2 collective-permute-done.39
  170.7 16.3 %attend.4 = (f32[128,512]{1,0:T(8,128)S(1)}, f32[128,512]{1,0:T(8,128)S(1)}, f32[128,1024]{1,0:T(8,128)S(1)}) custom-call(s32[3]{0:T(128)S(1)} %pad_add_fusion.info_ref, bf16[128,512]{1,0:T(8,128)(2,1)S(1)} %convolution_convert_fusion.1.mine_ref, bf16[128,512]{1,0:T(8,128)(2,1)S(1)} %collective-permute-done.40.other_ref, ...), custom_call_target="tpu_custom_call" | custom-call | flops 8589934592 | bytes 16777216 | tf_op jit(solution)/shard_map/attend/pallas_call | solution.py:367
  187.1 1.9 collective-permute-done.42
  190.7 2.5 collective-permute-done.43
  195.2 2.0 collective-permute-start.48
  197.2 2.0 collective-permute-start.49
  200.6 4.2 %collective-permute-done.44 = bf16[4,8,6144]{2,1,0:T(8,128)(2,1)S(1)} collective-permute-done((bf16[4,8,6144]{2,1,0:T(8,128)(2,1)S(1)}, bf16[4,8,6144]{2,1,0:T(8,128)(2,1)S(1)}, u32[]{:S(2)}, u32[]{:S(2)}) %collective-permute-start.44) | collective-permute-done | bytes 393248 | tf_op jit(solution)/shard_map/ppermute | solution.py:22
  206.6 2.0 collective-permute-start.45
  208.6 1.9 collective-permute-start.46
  212.3 6.6 %collective-permute-done.46 = bf16[8,6144]{1,0:T(8,128)(2,1)S(1)} collective-permute-done((bf16[8,6144]{1,0:T(8,128)(2,1)S(1)}, bf16[8,6144]{1,0:T(8,128)(2,1)S(1)}, u32[]{:S(2)}, u32[]{:S(2)}) %collective-permute-start.46) | collective-permute-done | bytes 98336 | tf_op jit(solution)/shard_map/ppermute | solution.py:505
  219.9 2.5 collective-permute-start.52
  224.3 1.9 collective-permute-start.57
  227.4 1.6 collective-permute-done.52
  229.0 2.5 collective-permute-start.59
  231.6 1.6 collective-permute-start.55
  233.1 3.7 %collective-permute-done.57 = bf16[2,8,3072]{2,1,0:T(8,128)(2,1)S(1)} collective-permute-done((bf16[2,8,3072]{2,1,0:T(8,128)(2,1)S(1)}, bf16[2,8,3072]{2,1,0:T(8,128)(2,1)S(1)}, u32[]{:S(2)}, u32[]{:S(2)}) %collective-permute-start.57) | collective-permute-done | bytes 98336 | tf_op jit(solution)/shard_map/ppermute | solution.py:505
  236.9 1.8 collective-permute-done.55
  239.3 2.5 collective-permute-done.60
  245.8 15.7 %attend.5 = (f32[128,512]{1,0:T(8,128)S(1)}, f32[128,512]{1,0:T(8,128)S(1)}, f32[128,1024]{1,0:T(8,128)S(1)}) custom-call(s32[3]{0:T(128)S(1)} %pad_add_fusion.info_ref, bf16[128,512]{1,0:T(8,128)(2,1)S(1)} %convolution_convert_fusion.mine_ref, bf16[128,512]{1,0:T(8,128)(2,1)S(1)} %collective-permute-done.61.other_ref, ...), custom_call_target="tpu_custom_call" | custom-call | flops 8589934592 | bytes 16777216 | tf_op jit(solution)/shard_map/attend/pallas_call | solution.py:367
  261.5 1.9 collective-permute-done.63
  265.1 2.5 collective-permute-done.64
  268.1 1.6 collective-permute-start.65
  269.7 2.7 collective-permute-start.69
  275.0 4.3 %collective-permute-done.65 = bf16[4,8,6144]{2,1,0:T(8,128)(2,1)S(1)} collective-permute-done((bf16[4,8,6144]{2,1,0:T(8,128)(2,1)S(1)}, bf16[4,8,6144]{2,1,0:T(8,128)(2,1)S(1)}, u32[]{:S(2)}, u32[]{:S(2)}) %collective-permute-start.65) | collective-permute-done | bytes 393248 | tf_op jit(solution)/shard_map/ppermute | solution.py:22
  281.1 2.6 collective-permute-start.66
  287.3 6.0 %collective-permute-done.67 = bf16[8,6144]{1,0:T(8,128)(2,1)S(1)} collective-permute-done((bf16[8,6144]{1,0:T(8,128)(2,1)S(1)}, bf16[8,6144]{1,0:T(8,128)(2,1)S(1)}, u32[]{:S(2)}, u32[]{:S(2)}) %collective-permute-start.67) | collective-permute-done | bytes 98336 | tf_op jit(solution)/shard_map/ppermute | solution.py:505
  (222 shorter events, 63.3 us)
Async XLA Ops:
  16.5 9.8 %collective-permute-start = (f32[64,6144]{1,0:T(8,128)}, f32[64,6144]{1,0:T(8,128)}, u32[]{:S(2)}, u32[]{:S(2)}) collective-permute-start(f32[64,6144]{1,0:T(8,128)} %get-tuple-element.39), channel_id=1, source_target_pairs={{0,1},{1,0},{2,3},{3,2},{4,5},{5,4},{6,7},{7,6},{8,9},{9,8},{10,11... | collective-permute-start | bytes 4718600 | tf_op jit(solution)/shard_map/ppermute | solution.py:22
  29.2 12.3 %collective-permute-start.2 = (bf16[4,8,6144]{2,1,0:T(8,128)(2,1)S(1)}, bf16[4,8,6144]{2,1,0:T(8,128)(2,1)S(1)}, u32[]{:S(2)}, u32[]{:S(2)}) collective-permute-start(bf16[4,8,6144]{2,1,0:T(8,128)(2,1)S(1)} %fusion.5), channel_id=1, source_target_pairs={{0,2},{1,3},{2,0},{3,1},{4,6},{5,7},{6,4},{7,5},{8,10},{9,11},{10,... | collective-permute-start | bytes 1179656 | tf_op jit(solution)/shard_map/ppermute | solution.py:22
  32.0 10.9 %collective-permute-start.6 = (bf16[2,8,2048]{2,1,0:T(8,128)(2,1)S(1)}, bf16[2,8,2048]{2,1,0:T(8,128)(2,1)S(1)}, u32[]{:S(2)}, u32[]{:S(2)}) collective-permute-start(bf16[2,8,2048]{2,1,0:T(8,128)(2,1)S(1)} %get-tuple-element.100), channel_id=1, source_target_pairs={{0,4},{1,5},{2,6},{3,7},{4,0},{5,1},{6,2},{7,3},{8,12},{9,13},{10,... | collective-permute-start | bytes 196616 | tf_op jit(solution)/shard_map/ppermute | solution.py:505
  33.6 9.2 %collective-permute-start.7 = (bf16[2,8,2048]{2,1,0:T(8,128)(2,1)S(1)}, bf16[2,8,2048]{2,1,0:T(8,128)(2,1)S(1)}, u32[]{:S(2)}, u32[]{:S(2)}) collective-permute-start(bf16[2,8,2048]{2,1,0:T(8,128)(2,1)S(1)} %get-tuple-element.99), channel_id=1, source_target_pairs={{0,8},{1,9},{2,10},{3,11},{4,12},{5,13},{6,14},{7,15},{8,0},{9,1},... | collective-permute-start | bytes 196616 | tf_op jit(solution)/shard_map/ppermute | solution.py:505
  36.2 6.6 %collective-permute-start.8 = (bf16[2,8,2048]{2,1,0:T(8,128)(2,1)S(1)}, bf16[2,8,2048]{2,1,0:T(8,128)(2,1)S(1)}, u32[]{:S(2)}, u32[]{:S(2)}) collective-permute-start(bf16[2,8,2048]{2,1,0:T(8,128)(2,1)S(1)} %get-tuple-element.98), channel_id=1, source_target_pairs={{0,12},{1,13},{2,14},{3,15},{4,8},{5,9},{6,10},{7,11},{8,4},{9,5},... | collective-permute-start | bytes 196616 | tf_op jit(solution)/shard_map/ppermute | solution.py:505
  42.9 6.2 %collective-permute-start.9 = (bf16[8,2048]{1,0:T(8,128)(2,1)S(1)}, bf16[8,2048]{1,0:T(8,128)(2,1)S(1)}, u32[]{:S(2)}, u32[]{:S(2)}) collective-permute-start(bf16[8,2048]{1,0:T(8,128)(2,1)S(1)} %fusion.80), channel_id=1, source_target_pairs={{0,2},{1,3},{2,0},{3,1},{4,6},{5,7},{6,4},{7,5},{8,10},{9,11},{10,... | collective-permute-start | bytes 98312 | tf_op jit(solution)/shard_map/ppermute | solution.py:22
  44.7 5.6 %collective-permute-start.3 = (bf16[8,6144]{1,0:T(8,128)(2,1)S(1)}, bf16[8,6144]{1,0:T(8,128)(2,1)S(1)}, u32[]{:S(2)}, u32[]{:S(2)}) collective-permute-start(bf16[8,6144]{1,0:T(8,128)(2,1)S(1)} %get-tuple-element.88), channel_id=1, source_target_pairs={{0,4},{1,5},{2,6},{3,7},{4,0},{5,1},{6,2},{7,3},{8,12},{9,13},{10,... | collective-permute-start | bytes 294920 | tf_op jit(solution)/shard_map/ppermute | solution.py:505
  46.3 9.9 %collective-permute-start.4 = (bf16[8,6144]{1,0:T(8,128)(2,1)S(1)}, bf16[8,6144]{1,0:T(8,128)(2,1)S(1)}, u32[]{:S(2)}, u32[]{:S(2)}) collective-permute-start(bf16[8,6144]{1,0:T(8,128)(2,1)S(1)} %get-tuple-element.87), channel_id=1, source_target_pairs={{0,8},{1,9},{2,10},{3,11},{4,12},{5,13},{6,14},{7,15},{8,0},{9,1},... | collective-permute-start | bytes 294920 | tf_op jit(solution)/shard_map/ppermute | solution.py:505
  48.9 7.3 %collective-permute-start.5 = (bf16[8,6144]{1,0:T(8,128)(2,1)S(1)}, bf16[8,6144]{1,0:T(8,128)(2,1)S(1)}, u32[]{:S(2)}, u32[]{:S(2)}) collective-permute-start(bf16[8,6144]{1,0:T(8,128)(2,1)S(1)} %get-tuple-element.86), channel_id=1, source_target_pairs={{0,12},{1,13},{2,14},{3,15},{4,8},{5,9},{6,10},{7,11},{8,4},{9,5},... | collective-permute-start | bytes 294920 | tf_op jit(solution)/shard_map/ppermute | solution.py:505
  56.5 5.0 %collective-permute-start.14 = (bf16[8,3072]{1,0:T(8,128)(2,1)S(1)}, bf16[8,3072]{1,0:T(8,128)(2,1)S(1)}, u32[]{:S(2)}, u32[]{:S(2)}) collective-permute-start(bf16[8,3072]{1,0:T(8,128)(2,1)S(1)} %get-tuple-element.135), channel_id=1, source_target_pairs={{0,2},{1,3},{2,0},{3,1},{4,6},{5,7},{6,4},{7,5},{8,10},{9,11},{10,... | collective-permute-start | bytes 147464 | tf_op jit(solution)/shard_map/ppermute | solution.py:22
  57.2 9.0 %collective-permute-start.10 = (bf16[8,5120]{1,0:T(8,128)(2,1)S(1)}, bf16[8,5120]{1,0:T(8,128)(2,1)S(1)}, u32[]{:S(2)}, u32[]{:S(2)}) collective-permute-start(bf16[8,5120]{1,0:T(8,128)(2,1)S(1)} %slice.84), channel_id=1, source_target_pairs={{0,8},{1,9},{2,10},{3,11},{4,12},{5,13},{6,14},{7,15},{8,0},{9,1},... | collective-permute-start | bytes 245768 | tf_op jit(solution)/shard_map/ppermute | solution.py:505
  59.8 8.7 %collective-permute-start.11 = (bf16[8,5120]{1,0:T(8,128)(2,1)S(1)}, bf16[8,5120]{1,0:T(8,128)(2,1)S(1)}, u32[]{:S(2)}, u32[]{:S(2)}) collective-permute-start(bf16[8,5120]{1,0:T(8,128)(2,1)S(1)} %slice.84), channel_id=1, source_target_pairs={{0,4},{1,5},{2,6},{3,7},{4,0},{5,1},{6,2},{7,3},{8,12},{9,13},{10,... | collective-permute-start | bytes 245768 | tf_op jit(solution)/shard_map/ppermute | solution.py:505
  60.2 8.3 %collective-permute-start.12 = (bf16[8,5120]{1,0:T(8,128)(2,1)S(1)}, bf16[8,5120]{1,0:T(8,128)(2,1)S(1)}, u32[]{:S(2)}, u32[]{:S(2)}) collective-permute-start(bf16[8,5120]{1,0:T(8,128)(2,1)S(1)} %slice.84), channel_id=1, source_target_pairs={{0,12},{1,13},{2,14},{3,15},{4,8},{5,9},{6,10},{7,11},{8,4},{9,5},... | collective-permute-start | bytes 245768 | tf_op jit(solution)/shard_map/ppermute | solution.py:505
  61.6 12.4 %collective-permute-start.15 = (bf16[2,8,3072]{2,1,0:T(8,128)(2,1)S(1)}, bf16[2,8,3072]{2,1,0:T(8,128)(2,1)S(1)}, u32[]{:S(2)}, u32[]{:S(2)}) collective-permute-start(bf16[2,8,3072]{2,1,0:T(8,128)(2,1)S(1)} %maximum_select_fusion.6), channel_id=1, source_target_pairs={{0,8},{1,9},{2,10},{3,11},{4,12},{5,13},{6,14},{7,15},{8,0},{9,1},... | collective-permute-start | bytes 294920 | tf_op jit(solution)/shard_map/ppermute | solution.py:505
  63.4 10.5 %collective-permute-start.16 = (bf16[2,8,3072]{2,1,0:T(8,128)(2,1)S(1)}, bf16[2,8,3072]{2,1,0:T(8,128)(2,1)S(1)}, u32[]{:S(2)}, u32[]{:S(2)}) collective-permute-start(bf16[2,8,3072]{2,1,0:T(8,128)(2,1)S(1)} %maximum_select_fusion.6), channel_id=1, source_target_pairs={{0,4},{1,5},{2,6},{3,7},{4,0},{5,1},{6,2},{7,3},{8,12},{9,13},{10,... | collective-permute-start | bytes 294920 | tf_op jit(solution)/shard_map/ppermute | solution.py:505
  66.2 7.8 %collective-permute-start.17 = (bf16[2,8,3072]{2,1,0:T(8,128)(2,1)S(1)}, bf16[2,8,3072]{2,1,0:T(8,128)(2,1)S(1)}, u32[]{:S(2)}, u32[]{:S(2)}) collective-permute-start(bf16[2,8,3072]{2,1,0:T(8,128)(2,1)S(1)} %maximum_select_fusion.6), channel_id=1, source_target_pairs={{0,12},{1,13},{2,14},{3,15},{4,8},{5,9},{6,10},{7,11},{8,4},{9,5},... | collective-permute-start | bytes 294920 | tf_op jit(solution)/shard_map/ppermute | solution.py:505
  68.6 7.1 %collective-permute-start.13 = (bf16[4,8,5120]{2,1,0:T(8,128)(2,1)S(1)}, bf16[4,8,5120]{2,1,0:T(8,128)(2,1)S(1)}, u32[]{:S(2)}, u32[]{:S(2)}) collective-permute-start(bf16[4,8,5120]{2,1,0:T(8,128)(2,1)S(1)} %get-tuple-element.129), channel_id=1, source_target_pairs={{0,2},{1,3},{2,0},{3,1},{4,6},{5,7},{6,4},{7,5},{8,10},{9,11},{10,... | collective-permute-start | bytes 983048 | tf_op jit(solution)/shard_map/ppermute | solution.py:22
  76.9 3.0 %collective-permute-start.18 = (bf16[4,2,8,8192]{3,2,1,0:T(8,128)(2,1)}, bf16[4,2,8,8192]{3,2,1,0:T(8,128)(2,1)}, u32[]{:S(2)}, u32[]{:S(2)}) collective-permute-start(bf16[4,2,8,8192]{3,2,1,0:T(8,128)(2,1)} %maximum_maximum_fusion), channel_id=1, source_target_pairs={{0,1},{1,0},{2,3},{3,2},{4,5},{5,4},{6,7},{7,6},{8,9},{9,8},{10,11... | collective-permute-start | bytes 3145736 | tf_op jit(solution)/shard_map/ppermute | solution.py:22
  86.3 2.2 collective-permute-start.19
  113.3 2.9 collective-permute-start.22
  118.5 11.2 %collective-permute-start.23 = (bf16[4,8,6144]{2,1,0:T(8,128)(2,1)S(1)}, bf16[4,8,6144]{2,1,0:T(8,128)(2,1)S(1)}, u32[]{:S(2)}, u32[]{:S(2)}) collective-permute-start(bf16[4,8,6144]{2,1,0:T(8,128)(2,1)S(1)} %fusion.6), channel_id=1, source_target_pairs={{0,2},{1,3},{2,0},{3,1},{4,6},{5,7},{6,4},{7,5},{8,10},{9,11},{10,... | collective-permute-start | bytes 1179656 | tf_op jit(solution)/shard_map/ppermute | solution.py:22
  120.1 9.8 %collective-permute-start.27 = (bf16[2,8,2048]{2,1,0:T(8,128)(2,1)S(1)}, bf16[2,8,2048]{2,1,0:T(8,128)(2,1)S(1)}, u32[]{:S(2)}, u32[]{:S(2)}) collective-permute-start(bf16[2,8,2048]{2,1,0:T(8,128)(2,1)S(1)} %get-tuple-element.97), channel_id=1, source_target_pairs={{0,4},{1,5},{2,6},{3,7},{4,0},{5,1},{6,2},{7,3},{8,12},{9,13},{10,... | collective-permute-start | bytes 196616 | tf_op jit(solution)/shard_map/ppermute | solution.py:505
  123.2 8.0 %collective-permute-start.28 = (bf16[2,8,2048]{2,1,0:T(8,128)(2,1)S(1)}, bf16[2,8,2048]{2,1,0:T(8,128)(2,1)S(1)}, u32[]{:S(2)}, u32[]{:S(2)}) collective-permute-start(bf16[2,8,2048]{2,1,0:T(8,128)(2,1)S(1)} %get-tuple-element.96), channel_id=1, source_target_pairs={{0,8},{1,9},{2,10},{3,11},{4,12},{5,13},{6,14},{7,15},{8,0},{9,1},... | collective-permute-start | bytes 196616 | tf_op jit(solution)/shard_map/ppermute | solution.py:505
  124.0 7.1 %collective-permute-start.29 = (bf16[2,8,2048]{2,1,0:T(8,128)(2,1)S(1)}, bf16[2,8,2048]{2,1,0:T(8,128)(2,1)S(1)}, u32[]{:S(2)}, u32[]{:S(2)}) collective-permute-start(bf16[2,8,2048]{2,1,0:T(8,128)(2,1)S(1)} %get-tuple-element.95), channel_id=1, source_target_pairs={{0,12},{1,13},{2,14},{3,15},{4,8},{5,9},{6,10},{7,11},{8,4},{9,5},... | collective-permute-start | bytes 196616 | tf_op jit(solution)/shard_map/ppermute | solution.py:505
  131.2 5.7 %collective-permute-start.30 = (bf16[8,2048]{1,0:T(8,128)(2,1)S(1)}, bf16[8,2048]{1,0:T(8,128)(2,1)S(1)}, u32[]{:S(2)}, u32[]{:S(2)}) collective-permute-start(bf16[8,2048]{1,0:T(8,128)(2,1)S(1)} %fusion.81), channel_id=1, source_target_pairs={{0,2},{1,3},{2,0},{3,1},{4,6},{5,7},{6,4},{7,5},{8,10},{9,11},{10,... | collective-permute-start | bytes 98312 | tf_op jit(solution)/shard_map/ppermute | solution.py:22
  131.8 6.1 %collective-permute-start.24 = (bf16[8,6144]{1,0:T(8,128)(2,1)S(1)}, bf16[8,6144]{1,0:T(8,128)(2,1)S(1)}, u32[]{:S(2)}, u32[]{:S(2)}) collective-permute-start(bf16[8,6144]{1,0:T(8,128)(2,1)S(1)} %get-tuple-element.85), channel_id=1, source_target_pairs={{0,4},{1,5},{2,6},{3,7},{4,0},{5,1},{6,2},{7,3},{8,12},{9,13},{10,... | collective-permute-start | bytes 294920 | tf_op jit(solution)/shard_map/ppermute | solution.py:505
  134.5 9.6 %collective-permute-start.25 = (bf16[8,6144]{1,0:T(8,128)(2,1)S(1)}, bf16[8,6144]{1,0:T(8,128)(2,1)S(1)}, u32[]{:S(2)}, u32[]{:S(2)}) collective-permute-start(bf16[8,6144]{1,0:T(8,128)(2,1)S(1)} %get-tuple-element.84), channel_id=1, source_target_pairs={{0,8},{1,9},{2,10},{3,11},{4,12},{5,13},{6,14},{7,15},{8,0},{9,1},... | collective-permute-start | bytes 294920 | tf_op jit(solution)/shard_map/ppermute | solution.py:505
  135.3 8.8 %collective-permute-start.26 = (bf16[8,6144]{1,0:T(8,128)(2,1)S(1)}, bf16[8,6144]{1,0:T(8,128)(2,1)S(1)}, u32[]{:S(2)}, u32[]{:S(2)}) collective-permute-start(bf16[8,6144]{1,0:T(8,128)(2,1)S(1)} %get-tuple-element.83), channel_id=1, source_target_pairs={{0,12},{1,13},{2,14},{3,15},{4,8},{5,9},{6,10},{7,11},{8,4},{9,5},... | collective-permute-start | bytes 294920 | tf_op jit(solution)/shard_map/ppermute | solution.py:505
  144.5 5.0 %collective-permute-start.35 = (bf16[8,3072]{1,0:T(8,128)(2,1)S(1)}, bf16[8,3072]{1,0:T(8,128)(2,1)S(1)}, u32[]{:S(2)}, u32[]{:S(2)}) collective-permute-start(bf16[8,3072]{1,0:T(8,128)(2,1)S(1)} %get-tuple-element.133), channel_id=1, source_target_pairs={{0,2},{1,3},{2,0},{3,1},{4,6},{5,7},{6,4},{7,5},{8,10},{9,11},{10,... | collective-permute-start | bytes 147464 | tf_op jit(solution)/shard_map/ppermute | solution.py:22
  145.1 7.6 %collective-permute-start.31 = (bf16[8,5120]{1,0:T(8,128)(2,1)S(1)}, bf16[8,5120]{1,0:T(8,128)(2,1)S(1)}, u32[]{:S(2)}, u32[]{:S(2)}) collective-permute-start(bf16[8,5120]{1,0:T(8,128)(2,1)S(1)} %slice.90), channel_id=1, source_target_pairs={{0,8},{1,9},{2,10},{3,11},{4,12},{5,13},{6,14},{7,15},{8,0},{9,1},... | collective-permute-start | bytes 245768 | tf_op jit(solution)/shard_map/ppermute | solution.py:505
  147.5 8.9 %collective-permute-start.32 = (bf16[8,5120]{1,0:T(8,128)(2,1)S(1)}, bf16[8,5120]{1,0:T(8,128)(2,1)S(1)}, u32[]{:S(2)}, u32[]{:S(2)}) collective-permute-start(bf16[8,5120]{1,0:T(8,128)(2,1)S(1)} %slice.90), channel_id=1, source_target_pairs={{0,4},{1,5},{2,6},{3,7},{4,0},{5,1},{6,2},{7,3},{8,12},{9,13},{10,... | collective-permute-start | bytes 245768 | tf_op jit(solution)/shard_map/ppermute | solution.py:505
  147.6 8.8 %collective-permute-start.33 = (bf16[8,5120]{1,0:T(8,128)(2,1)S(1)}, bf16[8,5120]{1,0:T(8,128)(2,1)S(1)}, u32[]{:S(2)}, u32[]{:S(2)}) collective-permute-start(bf16[8,5120]{1,0:T(8,128)(2,1)S(1)} %slice.90), channel_id=1, source_target_pairs={{0,12},{1,13},{2,14},{3,15},{4,8},{5,9},{6,10},{7,11},{8,4},{9,5},... | collective-permute-start | bytes 245768 | tf_op jit(solution)/shard_map/ppermute | solution.py:505
  149.5 12.1 %collective-permute-start.36 = (bf16[2,8,3072]{2,1,0:T(8,128)(2,1)S(1)}, bf16[2,8,3072]{2,1,0:T(8,128)(2,1)S(1)}, u32[]{:S(2)}, u32[]{:S(2)}) collective-permute-start(bf16[2,8,3072]{2,1,0:T(8,128)(2,1)S(1)} %maximum_select_fusion.7), channel_id=1, source_target_pairs={{0,8},{1,9},{2,10},{3,11},{4,12},{5,13},{6,14},{7,15},{8,0},{9,1},... | collective-permute-start | bytes 294920 | tf_op jit(solution)/shard_map/ppermute | solution.py:505
  151.1 10.5 %collective-permute-start.37 = (bf16[2,8,3072]{2,1,0:T(8,128)(2,1)S(1)}, bf16[2,8,3072]{2,1,0:T(8,128)(2,1)S(1)}, u32[]{:S(2)}, u32[]{:S(2)}) collective-permute-start(bf16[2,8,3072]{2,1,0:T(8,128)(2,1)S(1)} %maximum_select_fusion.7), channel_id=1, source_target_pairs={{0,4},{1,5},{2,6},{3,7},{4,0},{5,1},{6,2},{7,3},{8,12},{9,13},{10,... | collective-permute-start | bytes 294920 | tf_op jit(solution)/shard_map/ppermute | solution.py:505
  152.7 8.9 %collective-permute-start.38 = (bf16[2,8,3072]{2,1,0:T(8,128)(2,1)S(1)}, bf16[2,8,3072]{2,1,0:T(8,128)(2,1)S(1)}, u32[]{:S(2)}, u32[]{:S(2)}) collective-permute-start(bf16[2,8,3072]{2,1,0:T(8,128)(2,1)S(1)} %maximum_select_fusion.7), channel_id=1, source_target_pairs={{0,12},{1,13},{2,14},{3,15},{4,8},{5,9},{6,10},{7,11},{8,4},{9,5},... | collective-permute-start | bytes 294920 | tf_op jit(solution)/shard_map/ppermute | solution.py:505
  156.5 7.1 %collective-permute-start.34 = (bf16[4,8,5120]{2,1,0:T(8,128)(2,1)S(1)}, bf16[4,8,5120]{2,1,0:T(8,128)(2,1)S(1)}, u32[]{:S(2)}, u32[]{:S(2)}) collective-permute-start(bf16[4,8,5120]{2,1,0:T(8,128)(2,1)S(1)} %get-tuple-element.127), channel_id=1, source_target_pairs={{0,2},{1,3},{2,0},{3,1},{4,6},{5,7},{6,4},{7,5},{8,10},{9,11},{10,... | collective-permute-start | bytes 983048 | tf_op jit(solution)/shard_map/ppermute | solution.py:22
  164.0 2.7 collective-permute-start.39
  190.5 2.7 collective-permute-start.43
  193.7 11.2 %collective-permute-start.44 = (bf16[4,8,6144]{2,1,0:T(8,128)(2,1)S(1)}, bf16[4,8,6144]{2,1,0:T(8,128)(2,1)S(1)}, u32[]{:S(2)}, u32[]{:S(2)}) collective-permute-start(bf16[4,8,6144]{2,1,0:T(8,128)(2,1)S(1)} %fusion.7), channel_id=1, source_target_pairs={{0,2},{1,3},{2,0},{3,1},{4,6},{5,7},{6,4},{7,5},{8,10},{9,11},{10,... | collective-permute-start | bytes 1179656 | tf_op jit(solution)/shard_map/ppermute | solution.py:22
  195.2 9.8 %collective-permute-start.48 = (bf16[2,8,2048]{2,1,0:T(8,128)(2,1)S(1)}, bf16[2,8,2048]{2,1,0:T(8,128)(2,1)S(1)}, u32[]{:S(2)}, u32[]{:S(2)}) collective-permute-start(bf16[2,8,2048]{2,1,0:T(8,128)(2,1)S(1)} %get-tuple-element.94), channel_id=1, source_target_pairs={{0,4},{1,5},{2,6},{3,7},{4,0},{5,1},{6,2},{7,3},{8,12},{9,13},{10,... | collective-permute-start | bytes 196616 | tf_op jit(solution)/shard_map/ppermute | solution.py:505
  197.2 8.5 %collective-permute-start.49 = (bf16[2,8,2048]{2,1,0:T(8,128)(2,1)S(1)}, bf16[2,8,2048]{2,1,0:T(8,128)(2,1)S(1)}, u32[]{:S(2)}, u32[]{:S(2)}) collective-permute-start(bf16[2,8,2048]{2,1,0:T(8,128)(2,1)S(1)} %get-tuple-element.93), channel_id=1, source_target_pairs={{0,8},{1,9},{2,10},{3,11},{4,12},{5,13},{6,14},{7,15},{8,0},{9,1},... | collective-permute-start | bytes 196616 | tf_op jit(solution)/shard_map/ppermute | solution.py:505
  199.2 6.5 %collective-permute-start.50 = (bf16[2,8,2048]{2,1,0:T(8,128)(2,1)S(1)}, bf16[2,8,2048]{2,1,0:T(8,128)(2,1)S(1)}, u32[]{:S(2)}, u32[]{:S(2)}) collective-permute-start(bf16[2,8,2048]{2,1,0:T(8,128)(2,1)S(1)} %get-tuple-element.92), channel_id=1, source_target_pairs={{0,12},{1,13},{2,14},{3,15},{4,8},{5,9},{6,10},{7,11},{8,4},{9,5},... | collective-permute-start | bytes 196616 | tf_op jit(solution)/shard_map/ppermute | solution.py:505
  205.8 6.2 %collective-permute-start.51 = (bf16[8,2048]{1,0:T(8,128)(2,1)S(1)}, bf16[8,2048]{1,0:T(8,128)(2,1)S(1)}, u32[]{:S(2)}, u32[]{:S(2)}) collective-permute-start(bf16[8,2048]{1,0:T(8,128)(2,1)S(1)} %fusion.82), channel_id=1, source_target_pairs={{0,2},{1,3},{2,0},{3,1},{4,6},{5,7},{6,4},{7,5},{8,10},{9,11},{10,... | collective-permute-start | bytes 98312 | tf_op jit(solution)/shard_map/ppermute | solution.py:22
  206.6 5.7 %collective-permute-start.45 = (bf16[8,6144]{1,0:T(8,128)(2,1)S(1)}, bf16[8,6144]{1,0:T(8,128)(2,1)S(1)}, u32[]{:S(2)}, u32[]{:S(2)}) collective-permute-start(bf16[8,6144]{1,0:T(8,128)(2,1)S(1)} %get-tuple-element.82), channel_id=1, source_target_pairs={{0,4},{1,5},{2,6},{3,7},{4,0},{5,1},{6,2},{7,3},{8,12},{9,13},{10,... | collective-permute-start | bytes 294920 | tf_op jit(solution)/shard_map/ppermute | solution.py:505
  208.6 10.3 %collective-permute-start.46 = (bf16[8,6144]{1,0:T(8,128)(2,1)S(1)}, bf16[8,6144]{1,0:T(8,128)(2,1)S(1)}, u32[]{:S(2)}, u32[]{:S(2)}) collective-permute-start(bf16[8,6144]{1,0:T(8,128)(2,1)S(1)} %get-tuple-element.81), channel_id=1, source_target_pairs={{0,8},{1,9},{2,10},{3,11},{4,12},{5,13},{6,14},{7,15},{8,0},{9,1},... | collective-permute-start | bytes 294920 | tf_op jit(solution)/shard_map/ppermute | solution.py:505
  210.5 8.4 %collective-permute-start.47 = (bf16[8,6144]{1,0:T(8,128)(2,1)S(1)}, bf16[8,6144]{1,0:T(8,128)(2,1)S(1)}, u32[]{:S(2)}, u32[]{:S(2)}) collective-permute-start(bf16[8,6144]{1,0:T(8,128)(2,1)S(1)} %get-tuple-element.80), channel_id=1, source_target_pairs={{0,12},{1,13},{2,14},{3,15},{4,8},{5,9},{6,10},{7,11},{8,4},{9,5},... | collective-permute-start | bytes 294920 | tf_op jit(solution)/shard_map/ppermute | solution.py:505
  219.3 5.0 %collective-permute-start.56 = (bf16[8,3072]{1,0:T(8,128)(2,1)S(1)}, bf16[8,3072]{1,0:T(8,128)(2,1)S(1)}, u32[]{:S(2)}, u32[]{:S(2)}) collective-permute-start(bf16[8,3072]{1,0:T(8,128)(2,1)S(1)} %get-tuple-element.131), channel_id=1, source_target_pairs={{0,2},{1,3},{2,0},{3,1},{4,6},{5,7},{6,4},{7,5},{8,10},{9,11},{10,... | collective-permute-start | bytes 147464 | tf_op jit(solution)/shard_map/ppermute | solution.py:22
  219.9 9.1 %collective-permute-start.52 = (bf16[8,5120]{1,0:T(8,128)(2,1)S(1)}, bf16[8,5120]{1,0:T(8,128)(2,1)S(1)}, u32[]{:S(2)}, u32[]{:S(2)}) collective-permute-start(bf16[8,5120]{1,0:T(8,128)(2,1)S(1)} %slice.97), channel_id=1, source_target_pairs={{0,8},{1,9},{2,10},{3,11},{4,12},{5,13},{6,14},{7,15},{8,0},{9,1},... | collective-permute-start | bytes 245768 | tf_op jit(solution)/shard_map/ppermute | solution.py:505
  222.5 9.0 %collective-permute-start.53 = (bf16[8,5120]{1,0:T(8,128)(2,1)S(1)}, bf16[8,5120]{1,0:T(8,128)(2,1)S(1)}, u32[]{:S(2)}, u32[]{:S(2)}) collective-permute-start(bf16[8,5120]{1,0:T(8,128)(2,1)S(1)} %slice.97), channel_id=1, source_target_pairs={{0,4},{1,5},{2,6},{3,7},{4,0},{5,1},{6,2},{7,3},{8,12},{9,13},{10,... | collective-permute-start | bytes 245768 | tf_op jit(solution)/shard_map/ppermute | solution.py:505
  222.9 8.6 %collective-permute-start.54 = (bf16[8,5120]{1,0:T(8,128)(2,1)S(1)}, bf16[8,5120]{1,0:T(8,128)(2,1)S(1)}, u32[]{:S(2)}, u32[]{:S(2)}) collective-permute-start(bf16[8,5120]{1,0:T(8,128)(2,1)S(1)} %slice.97), channel_id=1, source_target_pairs={{0,12},{1,13},{2,14},{3,15},{4,8},{5,9},{6,10},{7,11},{8,4},{9,5},... | collective-permute-start | bytes 245768 | tf_op jit(solution)/shard_map/ppermute | solution.py:505
  224.3 12.5 %collective-permute-start.57 = (bf16[2,8,3072]{2,1,0:T(8,128)(2,1)S(1)}, bf16[2,8,3072]{2,1,0:T(8,128)(2,1)S(1)}, u32[]{:S(2)}, u32[]{:S(2)}) collective-permute-start(bf16[2,8,3072]{2,1,0:T(8,128)(2,1)S(1)} %maximum_select_fusion.8), channel_id=1, source_target_pairs={{0,8},{1,9},{2,10},{3,11},{4,12},{5,13},{6,14},{7,15},{8,0},{9,1},... | collective-permute-start | bytes 294920 | tf_op jit(solution)/shard_map/ppermute | solution.py:505
  226.2 10.7 %collective-permute-start.58 = (bf16[2,8,3072]{2,1,0:T(8,128)(2,1)S(1)}, bf16[2,8,3072]{2,1,0:T(8,128)(2,1)S(1)}, u32[]{:S(2)}, u32[]{:S(2)}) collective-permute-start(bf16[2,8,3072]{2,1,0:T(8,128)(2,1)S(1)} %maximum_select_fusion.8), channel_id=1, source_target_pairs={{0,4},{1,5},{2,6},{3,7},{4,0},{5,1},{6,2},{7,3},{8,12},{9,13},{10,... | collective-permute-start | bytes 294920 | tf_op jit(solution)/shard_map/ppermute | solution.py:505
  229.0 7.9 %collective-permute-start.59 = (bf16[2,8,3072]{2,1,0:T(8,128)(2,1)S(1)}, bf16[2,8,3072]{2,1,0:T(8,128)(2,1)S(1)}, u32[]{:S(2)}, u32[]{:S(2)}) collective-permute-start(bf16[2,8,3072]{2,1,0:T(8,128)(2,1)S(1)} %maximum_select_fusion.8), channel_id=1, source_target_pairs={{0,12},{1,13},{2,14},{3,15},{4,8},{5,9},{6,10},{7,11},{8,4},{9,5},... | collective-permute-start | bytes 294920 | tf_op jit(solution)/shard_map/ppermute | solution.py:505
  231.6 7.1 %collective-permute-start.55 = (bf16[4,8,5120]{2,1,0:T(8,128)(2,1)S(1)}, bf16[4,8,5120]{2,1,0:T(8,128)(2,1)S(1)}, u32[]{:S(2)}, u32[]{:S(2)}) collective-permute-start(bf16[4,8,5120]{2,1,0:T(8,128)(2,1)S(1)} %get-tuple-element.125), channel_id=1, source_target_pairs={{0,2},{1,3},{2,0},{3,1},{4,6},{5,7},{6,4},{7,5},{8,10},{9,11},{10,... | collective-permute-start | bytes 983048 | tf_op jit(solution)/shard_map/ppermute | solution.py:22
  239.1 2.7 collective-permute-start.60
  264.9 2.7 collective-permute-start.64
  268.1 11.2 %collective-permute-start.65 = (bf16[4,8,6144]{2,1,0:T(8,128)(2,1)S(1)}, bf16[4,8,6144]{2,1,0:T(8,128)(2,1)S(1)}, u32[]{:S(2)}, u32[]{:S(2)}) collective-permute-start(bf16[4,8,6144]{2,1,0:T(8,128)(2,1)S(1)} %fusion.8), channel_id=1, source_target_pairs={{0,2},{1,3},{2,0},{3,1},{4,6},{5,7},{6,4},{7,5},{8,10},{9,11},{10,... | collective-permute-start | bytes 1179656 | tf_op jit(solution)/shard_map/ppermute | solution.py:22
  269.7 9.8 %collective-permute-start.69 = (bf16[2,8,2048]{2,1,0:T(8,128)(2,1)S(1)}, bf16[2,8,2048]{2,1,0:T(8,128)(2,1)S(1)}, u32[]{:S(2)}, u32[]{:S(2)}) collective-permute-start(bf16[2,8,2048]{2,1,0:T(8,128)(2,1)S(1)} %get-tuple-element.91), channel_id=1, source_target_pairs={{0,4},{1,5},{2,6},{3,7},{4,0},{5,1},{6,2},{7,3},{8,12},{9,13},{10,... | collective-permute-start | bytes 196616 | tf_op jit(solution)/shard_map/ppermute | solution.py:505
  272.4 8.1 %collective-permute-start.70 = (bf16[2,8,2048]{2,1,0:T(8,128)(2,1)S(1)}, bf16[2,8,2048]{2,1,0:T(8,128)(2,1)S(1)}, u32[]{:S(2)}, u32[]{:S(2)}) collective-permute-start(bf16[2,8,2048]{2,1,0:T(8,128)(2,1)S(1)} %get-tuple-element.90), channel_id=1, source_target_pairs={{0,8},{1,9},{2,10},{3,11},{4,12},{5,13},{6,14},{7,15},{8,0},{9,1},... | collective-permute-start | bytes 196616 | tf_op jit(solution)/shard_map/ppermute | solution.py:505
  273.6 6.8 %collective-permute-start.71 = (bf16[2,8,2048]{2,1,0:T(8,128)(2,1)S(1)}, bf16[2,8,2048]{2,1,0:T(8,128)(2,1)S(1)}, u32[]{:S(2)}, u32[]{:S(2)}) collective-permute-start(bf16[2,8,2048]{2,1,0:T(8,128)(2,1)S(1)} %get-tuple-element.89), channel_id=1, source_target_pairs={{0,12},{1,13},{2,14},{3,15},{4,8},{5,9},{6,10},{7,11},{8,4},{9,5},... | collective-permute-start | bytes 196616 | tf_op jit(solution)/shard_map/ppermute | solution.py:505
  280.5 5.8 %collective-permute-start.72 = (bf16[8,2048]{1,0:T(8,128)(2,1)S(1)}, bf16[8,2048]{1,0:T(8,128)(2,1)S(1)}, u32[]{:S(2)}, u32[]{:S(2)}) collective-permute-start(bf16[8,2048]{1,0:T(8,128)(2,1)S(1)} %fusion.83), channel_id=1, source_target_pairs={{0,2},{1,3},{2,0},{3,1},{4,6},{5,7},{6,4},{7,5},{8,10},{9,11},{10,... | collective-permute-start | bytes 98312 | tf_op jit(solution)/shard_map/ppermute | solution.py:22
  281.1 6.2 %collective-permute-start.66 = (bf16[8,6144]{1,0:T(8,128)(2,1)S(1)}, bf16[8,6144]{1,0:T(8,128)(2,1)S(1)}, u32[]{:S(2)}, u32[]{:S(2)}) collective-permute-start(bf16[8,6144]{1,0:T(8,128)(2,1)S(1)} %get-tuple-element.79), channel_id=1, source_target_pairs={{0,4},{1,5},{2,6},{3,7},{4,0},{5,1},{6,2},{7,3},{8,12},{9,13},{10,... | collective-permute-start | bytes 294920 | tf_op jit(solution)/shard_map/ppermute | solution.py:505
  283.7 9.7 %collective-permute-start.67 = (bf16[8,6144]{1,0:T(8,128)(2,1)S(1)}, bf16[8,6144]{1,0:T(8,128)(2,1)S(1)}, u32[]{:S(2)}, u32[]{:S(2)}) collective-permute-start(bf16[8,6144]{1,0:T(8,128)(2,1)S(1)} %get-tuple-element.78), channel_id=1, source_target_pairs={{0,8},{1,9},{2,10},{3,11},{4,12},{5,13},{6,14},{7,15},{8,0},{9,1},... | collective-permute-start | bytes 294920 | tf_op jit(solution)/shard_map/ppermute | solution.py:505
  284.9 8.5 %collective-permute-start.68 = (bf16[8,6144]{1,0:T(8,128)(2,1)S(1)}, bf16[8,6144]{1,0:T(8,128)(2,1)S(1)}, u32[]{:S(2)}, u32[]{:S(2)}) collective-permute-start(bf16[8,6144]{1,0:T(8,128)(2,1)S(1)} %get-tuple-element.77), channel_id=1, source_target_pairs={{0,12},{1,13},{2,14},{3,15},{4,8},{5,9},{6,10},{7,11},{8,4},{9,5},... | collective-permute-start | bytes 294920 | tf_op jit(solution)/shard_map/ppermute | solution.py:505
  (24 other events, 231.5 us)
